TPU v7x, 32 devices: a whole 2x2x4 slice. The times are simulated.
32 devices in a mesh: dp: 8 (over z, x), fsdp: 4 (over y, core).
Axes of the slice: x: 2, y: 2, z: 4, core: 2. Of those that a mesh axis runs over, the one named last changes fastest.
Arguments:
- x_now: float32 [32768, 78], P(('dp', 'fsdp'))
- x_next: float32 [32768, 78], P(('dp', 'fsdp'))
- node_counts: int32 [64], P(('dp', 'fsdp')), may hold values from 138 to 512, as said below
- border_flag: int32 [32768], P(('dp', 'fsdp')), may hold values 0 or 1
- source_vertex: int32 [64, 3072], P(('dp', 'fsdp')), may hold values from 0 to 511, as said below
- target_vertex: int32 [64, 3072], P(('dp', 'fsdp')), may hold values from 0 to 511, as said below
- link_features: float32 [64, 3072, 4], P(('dp', 'fsdp')), may hold values from -5 to 5
- level_ids: int32 [78], replicated, may hold values from 0 to 12
- encoder: float32 [78, 256], P(None, 'fsdp'), may hold values from -0.625 to 0.625
- edge_encoder: float32 [4, 256], P(None, 'fsdp'), may hold values from -3 to 3
- edge_first: float32 [3, 768, 256], P(None, 'fsdp'), may hold values from -0.21875 to 0.21875
- second_layers: float32 [3, 2, 256, 256], P(None, None, 'fsdp'), may hold values from -0.375 to 0.375
- node_first: float32 [3, 512, 256], P(None, 'fsdp'), may hold values from -0.25 to 0.25
- vectors: float32 [3, 2, 4, 256], P(None, None, None, 'fsdp'), as said below
- decoder: float32 [256, 78], P('fsdp'), may hold values from -0.375 to 0.375
- encoder_moment: float32 [78, 256], P(None, 'fsdp'), may hold values from -9.1552734e-05 to 9.1552734e-05
- edge_encoder_moment: float32 [4, 256], P(None, 'fsdp'), may hold values from -9.1552734e-05 to 9.1552734e-05
- edge_first_moment: float32 [3, 768, 256], P(None, 'fsdp'), may hold values from -9.1552734e-05 to 9.1552734e-05
- second_layers_moment: float32 [3, 2, 256, 256], P(None, None, 'fsdp'), may hold values from -9.1552734e-05 to 9.1552734e-05
- node_first_moment: float32 [3, 512, 256], P(None, 'fsdp'), may hold values from -9.1552734e-05 to 9.1552734e-05
- vectors_moment: float32 [3, 2, 4, 256], P(None, None, None, 'fsdp'), may hold values from -9.1552734e-05 to 9.1552734e-05
- decoder_moment: float32 [256, 78], P('fsdp'), may hold values from -9.1552734e-05 to 9.1552734e-05
- encoder_square: float32 [78, 256], P(None, 'fsdp'), may hold values from 9.155413e-12 to 1.4648661e-10
- edge_encoder_square: float32 [4, 256], P(None, 'fsdp'), may hold values from 3.6621653e-10 to 1.23598077e-07
- edge_first_square: float32 [3, 768, 256], P(None, 'fsdp'), may hold values from 9.155413e-12 to 1.4648661e-10
- second_layers_square: float32 [3, 2, 256, 256], P(None, None, 'fsdp'), may hold values from 9.155413e-12 to 1.4648661e-10
- node_first_square: float32 [3, 512, 256], P(None, 'fsdp'), may hold values from 9.155413e-12 to 1.4648661e-10
- vectors_square: float32 [3, 2, 4, 256], P(None, None, None, 'fsdp'), may hold values from 9.155413e-12 to 1.4648661e-10
- decoder_square: float32 [256, 78], P('fsdp'), may hold values from 9.155413e-12 to 1.4648661e-10
Outputs:
- loss_sum: float32 [], replicated
- loss_count: float32 [], replicated
- encoder_moment_new: float32 [78, 256], P(None, 'fsdp')
- encoder_square_new: float32 [78, 256], P(None, 'fsdp')
- encoder_new: float32 [78, 256], P(None, 'fsdp')
- edge_encoder_moment_new: float32 [4, 256], P(None, 'fsdp')
- edge_encoder_square_new: float32 [4, 256], P(None, 'fsdp')
- edge_encoder_new: float32 [4, 256], P(None, 'fsdp')
- edge_first_moment_new: float32 [3, 768, 256], P(None, 'fsdp')
- edge_first_square_new: float32 [3, 768, 256], P(None, 'fsdp')
- edge_first_new: float32 [3, 768, 256], P(None, 'fsdp')
- second_layers_moment_new: float32 [3, 2, 256, 256], P(None, None, 'fsdp')
- second_layers_square_new: float32 [3, 2, 256, 256], P(None, None, 'fsdp')
- second_layers_new: float32 [3, 2, 256, 256], P(None, None, 'fsdp')
- node_first_moment_new: float32 [3, 512, 256], P(None, 'fsdp')
- node_first_square_new: float32 [3, 512, 256], P(None, 'fsdp')
- node_first_new: float32 [3, 512, 256], P(None, 'fsdp')
- vectors_moment_new: float32 [3, 2, 4, 256], P(None, None, None, 'fsdp')
- vectors_square_new: float32 [3, 2, 4, 256], P(None, None, None, 'fsdp')
- vectors_new: float32 [3, 2, 4, 256], P(None, None, None, 'fsdp')
- decoder_moment_new: float32 [256, 78], P('fsdp')
- decoder_square_new: float32 [256, 78], P('fsdp')
- decoder_new: float32 [256, 78], P('fsdp')
Inputs may be any that keep to these rules, and one draw needn't show every extreme that they name: `node_counts`: the last subgraph is full. `source_vertex`: every sender is a valid node of its subgraph. `target_vertex`: every receiver is a valid node of its subgraph. `vectors`: gains lie in 0.6 to 1.4.
All inputs are finite; a program needn't handle non-finite values. No bound on the sum of `border_flag` on one device may be relied on, other than what follows from the above.
Results may differ from a plain program's by a relative error of at most 0.0038.
The roundings to bfloat16 on the way count: a program that leaves them out, or rounds other values in their place, can miss the bound.
Values may be sent and summed in bfloat16 or wider, within the bound.
No kernel may reach another device: no remote copies, remote signals or barrier semaphores. Data moves between devices by JAX's collectives and lax.ppermute only.
A program may use at most 256 MiB of HBM per device.

v0:
```python
import jax
import jax.numpy as jnp
from jax import lax
from jax.sharding import PartitionSpec as P

VARS = 6
LEVELS = 13
ROUNDS = 3
STEP = 10


norm_eps = 1e-05
stat_eps = 1e-06
beta_one = 0.9
beta_two = 0.999
adam_eps = 1e-08
decay_rate = 0.01
rate_matrix = 0.03
rate_vector = 0.2


def to_low(value):
    return value.astype(jnp.bfloat16)


def one_hot(ids, count):
    return (ids[:, :, None] == jnp.arange(count, dtype=jnp.int32)[None, None, :]).astype(
        jnp.bfloat16
    )


def pick_rows(table, values):
    return jnp.einsum("sen,snd->sed", table, values, preferred_element_type=jnp.float32)


def spread_rows(table, values):
    return jnp.einsum("sen,sed->snd", table, values, preferred_element_type=jnp.float32)


def block_forward(feed_quantities, first, second, vector_rows):
    pre_one = jnp.dot(feed_quantities, first, preferred_element_type=jnp.float32) + vector_rows[0]
    active = to_low(jax.nn.silu(pre_one))
    pre_two = jnp.dot(active, second, preferred_element_type=jnp.float32) + vector_rows[1]
    centered = pre_two - jnp.mean(pre_two, axis=-1, keepdims=True)
    inverse = lax.rsqrt(jnp.mean(centered * centered, axis=-1, keepdims=True) + norm_eps)
    normed = centered * inverse
    return (normed * vector_rows[2] + vector_rows[3], (pre_one, active, normed, inverse))


def block_backward(grad_out, feed_quantities, first, second, vector_rows, stored):
    pre_one, active, normed, inverse = stored
    scaled = grad_out * vector_rows[2]
    grad_two = inverse * (
        scaled
        - jnp.mean(scaled, axis=-1, keepdims=True)
        - normed * jnp.mean(scaled * normed, axis=-1, keepdims=True)
    )
    low_two = to_low(grad_two)
    grad_second = jnp.einsum("rk,rd->kd", active, low_two, preferred_element_type=jnp.float32)
    grad_active = jnp.einsum("rd,kd->rk", low_two, second, preferred_element_type=jnp.float32)
    gate_value = jax.nn.sigmoid(pre_one)
    grad_one = grad_active * gate_value * (1.0 + pre_one * (1.0 - gate_value))
    low_one = to_low(grad_one)
    grad_first = jnp.einsum(
        "rk,rd->kd", feed_quantities, low_one, preferred_element_type=jnp.float32
    )
    grad_inputs = jnp.einsum("rd,kd->rk", low_one, first, preferred_element_type=jnp.float32)
    grad_rows = jnp.stack(
        [
            jnp.sum(low_one.astype(jnp.float32), axis=0),
            jnp.sum(low_two.astype(jnp.float32), axis=0),
            jnp.sum(grad_out * normed, axis=0),
            jnp.sum(grad_out, axis=0),
        ]
    )
    return (grad_inputs, grad_first, grad_second, grad_rows)


def round_forward(state, edge_state, link_reduced, send_table, recv_table, weights):
    edge_weight, second_pair, node_weight, vector_low = weights
    vector_rows = vector_low.astype(jnp.float32)
    graphs, node_count, latent = state.shape
    edge_count = edge_state.shape[1]
    node_low = to_low(state)
    from_send = to_low(pick_rows(send_table, node_low))
    from_recv = to_low(pick_rows(recv_table, node_low))
    edge_in = jnp.concatenate([from_send, from_recv, link_reduced], axis=-1).reshape(
        graphs * edge_count, 3 * latent
    )
    message, edge_stored = block_forward(edge_in, edge_weight, second_pair[0], vector_rows[0])
    edge_state = edge_state + message.reshape(graphs, edge_count, latent)
    link_reduced = to_low(edge_state)
    arriving_messages = to_low(spread_rows(recv_table, link_reduced))
    node_in = jnp.concatenate([node_low, arriving_messages], axis=-1).reshape(
        graphs * node_count, 2 * latent
    )
    update, node_stored = block_forward(node_in, node_weight, second_pair[1], vector_rows[1])
    state = state + update.reshape(graphs, node_count, latent)
    return (state, edge_state, link_reduced, (edge_in, edge_stored, node_in, node_stored))


def round_backward(grad_state, grad_edge, send_table, recv_table, weights, stored):
    edge_weight, second_pair, node_weight, vector_low = weights
    vector_rows = vector_low.astype(jnp.float32)
    edge_in, edge_stored, node_in, node_stored = stored
    graphs, node_count, latent = grad_state.shape
    edge_count = grad_edge.shape[1]
    grad_node_in, node_grad_first, node_grad_second, node_grad_rows = block_backward(
        grad_state.reshape(graphs * node_count, latent),
        node_in,
        node_weight,
        second_pair[1],
        vector_rows[1],
        node_stored,
    )
    grad_node_in = grad_node_in.reshape(graphs, node_count, 2 * latent)
    grad_incoming = to_low(grad_node_in[..., latent:])
    grad_edge = grad_edge + pick_rows(recv_table, grad_incoming)
    grad_edge_in, edge_grad_first, edge_grad_second, edge_grad_rows = block_backward(
        grad_edge.reshape(graphs * edge_count, latent),
        edge_in,
        edge_weight,
        second_pair[0],
        vector_rows[0],
        edge_stored,
    )
    grad_edge_in = grad_edge_in.reshape(graphs, edge_count, 3 * latent)
    grad_send = to_low(grad_edge_in[..., :latent])
    grad_recv = to_low(grad_edge_in[..., latent : 2 * latent])
    grad_state = (
        grad_state
        + grad_node_in[..., :latent]
        + spread_rows(send_table, grad_send)
        + spread_rows(recv_table, grad_recv)
    )
    grad_edge = grad_edge + grad_edge_in[..., 2 * latent :]
    gradients = (
        edge_grad_first,
        jnp.stack([edge_grad_second, node_grad_second]),
        node_grad_first,
        jnp.stack([edge_grad_rows, node_grad_rows]),
    )
    return (grad_state, grad_edge, gradients)


def adam_update(weight, moment, square, gradient, rate):
    moment_new = beta_one * moment + (1.0 - beta_one) * gradient
    square_new = beta_two * square + (1.0 - beta_two) * gradient * gradient
    direction = (
        moment_new
        / (1.0 - beta_one**STEP)
        / (jnp.sqrt(square_new / (1.0 - beta_two**STEP)) + adam_eps)
    )
    return (moment_new, square_new, weight - rate * (direction + decay_rate * weight))


def body(
    x_now,
    x_next,
    node_counts,
    border_flag,
    source_vertex,
    target_vertex,
    link_features,
    level_ids,
    encoder,
    edge_encoder,
    edge_first,
    second_layers,
    node_first,
    vectors,
    decoder,
    encoder_moment,
    edge_encoder_moment,
    edge_first_moment,
    second_layers_moment,
    node_first_moment,
    vectors_moment,
    decoder_moment,
    encoder_square,
    edge_encoder_square,
    edge_first_square,
    second_layers_square,
    node_first_square,
    vectors_square,
    decoder_square,
):
    graphs, edge_count = source_vertex.shape
    node_count = x_now.shape[0] // graphs
    channels = x_now.shape[1]
    latent = edge_first.shape[2]
    placeholder_places = jnp.arange(node_count, dtype=jnp.int32)
    valid = placeholder_places[None, :] < node_counts[:, None]
    driver_vector = border_flag.reshape(graphs, node_count) == 1
    genuine_flag = (
        jnp.where(valid & jnp.logical_not(driver_vector), 1.0, 0.0).astype(jnp.float32).reshape(-1)
    )
    tendency_increment = x_next - x_now
    feed_quantities = jnp.where(driver_vector.reshape(-1, 1), x_next, x_now)
    grouped = (tendency_increment * genuine_flag[:, None]).reshape(-1, VARS, LEVELS)
    local_sum = jnp.sum(grouped, axis=(0, 2))
    local_count = jnp.sum(genuine_flag)
    total_sum, total_count = lax.psum((local_sum, local_count), ("dp", "fsdp"))
    average = total_sum / (total_count * LEVELS)
    centered = (
        tendency_increment.reshape(-1, VARS, LEVELS) - average[None, :, None]
    ) * genuine_flag[:, None, None]
    spread = lax.psum(jnp.sum(centered * centered, axis=(0, 2)), ("dp", "fsdp"))
    variance = spread / (total_count * LEVELS)
    scale = jnp.repeat(lax.rsqrt(variance + stat_eps), LEVELS)
    level_weight = (level_ids.astype(jnp.float32) + 1.0) / LEVELS
    loss_count = total_count * channels
    encoder_full, edge_encoder_full, decoder_full = (
        lax.all_gather(to_low(encoder), "fsdp", axis=1, tiled=True),
        lax.all_gather(to_low(edge_encoder), "fsdp", axis=1, tiled=True),
        lax.all_gather(to_low(decoder), "fsdp", axis=0, tiled=True),
    )
    input_low = to_low(feed_quantities)
    state = jnp.dot(input_low, encoder_full, preferred_element_type=jnp.float32).reshape(
        graphs, node_count, latent
    )
    geometry_low = to_low(link_features.reshape(graphs * edge_count, -1))
    edge_state = jnp.dot(
        geometry_low, edge_encoder_full, preferred_element_type=jnp.float32
    ).reshape(graphs, edge_count, latent)
    link_reduced = to_low(edge_state)
    send_table = one_hot(source_vertex, node_count)
    recv_table = one_hot(target_vertex, node_count)
    stored_all = []
    weights_all = []
    for index_round in range(ROUNDS):
        weights = (
            lax.all_gather(to_low(edge_first[index_round]), "fsdp", axis=0, tiled=True),
            lax.all_gather(to_low(second_layers[index_round]), "fsdp", axis=1, tiled=True),
            lax.all_gather(to_low(node_first[index_round]), "fsdp", axis=0, tiled=True),
            lax.all_gather(to_low(vectors[index_round]), "fsdp", axis=2, tiled=True),
        )
        state, edge_state, link_reduced, stored = round_forward(
            state, edge_state, link_reduced, send_table, recv_table, weights
        )
        stored_all.append(stored)
        weights_all.append(weights)
    final_low = to_low(state.reshape(graphs * node_count, latent))
    predicted = jnp.dot(final_low, decoder_full, preferred_element_type=jnp.float32)
    misfit = (predicted - tendency_increment) * scale[None, :]
    weighting = level_weight[None, :] * genuine_flag[:, None]
    loss_sum = lax.psum(jnp.sum(weighting * misfit * misfit), ("dp", "fsdp"))
    grad_pred = to_low(2.0 * weighting * misfit * scale[None, :] / loss_count)
    grad_decoder = jnp.einsum("rk,rc->kc", final_low, grad_pred, preferred_element_type=jnp.float32)
    grad_state = jnp.einsum(
        "rc,kc->rk", grad_pred, decoder_full, preferred_element_type=jnp.float32
    ).reshape(graphs, node_count, latent)
    grad_edge = jnp.zeros((graphs, edge_count, latent), jnp.float32)
    round_grads = [None] * ROUNDS
    for index_round in reversed(range(ROUNDS)):
        weights = (
            lax.all_gather(to_low(edge_first[index_round]), "fsdp", axis=0, tiled=True),
            lax.all_gather(to_low(second_layers[index_round]), "fsdp", axis=1, tiled=True),
            lax.all_gather(to_low(node_first[index_round]), "fsdp", axis=0, tiled=True),
            lax.all_gather(to_low(vectors[index_round]), "fsdp", axis=2, tiled=True),
        )
        grad_state, grad_edge, gradients = round_backward(
            grad_state, grad_edge, send_table, recv_table, weights, stored_all[index_round]
        )
        owned_part = (
            lax.psum_scatter(gradients[0], "fsdp", scatter_dimension=0, tiled=True),
            lax.psum_scatter(gradients[1], "fsdp", scatter_dimension=1, tiled=True),
            lax.psum_scatter(gradients[2], "fsdp", scatter_dimension=0, tiled=True),
            lax.psum_scatter(gradients[3], "fsdp", scatter_dimension=2, tiled=True),
        )
        round_grads[index_round] = lax.psum(
            (owned_part[0], owned_part[1], owned_part[2], owned_part[3]), "dp"
        )
    grad_edge_low = to_low(grad_edge.reshape(graphs * edge_count, latent))
    grad_edge_encoder = jnp.einsum(
        "rf,rd->fd", geometry_low, grad_edge_low, preferred_element_type=jnp.float32
    )
    grad_encoder = jnp.einsum(
        "rc,rd->cd",
        input_low,
        to_low(grad_state.reshape(graphs * node_count, latent)),
        preferred_element_type=jnp.float32,
    )
    outer_part = (
        lax.psum_scatter(grad_encoder, "fsdp", scatter_dimension=1, tiled=True),
        lax.psum_scatter(grad_edge_encoder, "fsdp", scatter_dimension=1, tiled=True),
        lax.psum_scatter(grad_decoder, "fsdp", scatter_dimension=0, tiled=True),
    )
    outer_grads = lax.psum((outer_part[0], outer_part[1], outer_part[2]), "dp")
    gradients_all = (
        outer_grads[0],
        outer_grads[1],
        jnp.stack([round_grads[k][0] for k in range(ROUNDS)]),
        jnp.stack([round_grads[k][1] for k in range(ROUNDS)]),
        jnp.stack([round_grads[k][2] for k in range(ROUNDS)]),
        jnp.stack([round_grads[k][3] for k in range(ROUNDS)]),
        outer_grads[2],
    )
    params = (encoder, edge_encoder, edge_first, second_layers, node_first, vectors, decoder)
    moments = (
        encoder_moment,
        edge_encoder_moment,
        edge_first_moment,
        second_layers_moment,
        node_first_moment,
        vectors_moment,
        decoder_moment,
    )
    squares = (
        encoder_square,
        edge_encoder_square,
        edge_first_square,
        second_layers_square,
        node_first_square,
        vectors_square,
        decoder_square,
    )
    rates = (
        rate_matrix,
        rate_matrix,
        rate_matrix,
        rate_matrix,
        rate_matrix,
        rate_vector,
        rate_matrix,
    )
    results = [
        adam_update(params[k], moments[k], squares[k], gradients_all[k], rates[k]) for k in range(7)
    ]
    return (
        loss_sum,
        loss_count,
        results[0][0],
        results[0][1],
        results[0][2],
        results[1][0],
        results[1][1],
        results[1][2],
        results[2][0],
        results[2][1],
        results[2][2],
        results[3][0],
        results[3][1],
        results[3][2],
        results[4][0],
        results[4][1],
        results[4][2],
        results[5][0],
        results[5][1],
        results[5][2],
        results[6][0],
        results[6][1],
        results[6][2],
    )


def solution(mesh):
    placed = (
        P(("dp", "fsdp"), None),
        P(("dp", "fsdp"), None),
        P(("dp", "fsdp")),
        P(("dp", "fsdp")),
        P(("dp", "fsdp"), None),
        P(("dp", "fsdp"), None),
        P(("dp", "fsdp"), None, None),
        P(),
        P(None, "fsdp"),
        P(None, "fsdp"),
        P(None, "fsdp", None),
        P(None, None, "fsdp", None),
        P(None, "fsdp", None),
        P(None, None, None, "fsdp"),
        P("fsdp", None),
        P(None, "fsdp"),
        P(None, "fsdp"),
        P(None, "fsdp", None),
        P(None, None, "fsdp", None),
        P(None, "fsdp", None),
        P(None, None, None, "fsdp"),
        P("fsdp", None),
        P(None, "fsdp"),
        P(None, "fsdp"),
        P(None, "fsdp", None),
        P(None, None, "fsdp", None),
        P(None, "fsdp", None),
        P(None, None, None, "fsdp"),
        P("fsdp", None),
    )
    return jax.shard_map(
        body,
        mesh=mesh,
        in_specs=placed,
        out_specs=(
            P(),
            P(),
            P(None, "fsdp"),
            P(None, "fsdp"),
            P(None, "fsdp"),
            P(None, "fsdp"),
            P(None, "fsdp"),
            P(None, "fsdp"),
            P(None, "fsdp", None),
            P(None, "fsdp", None),
            P(None, "fsdp", None),
            P(None, None, "fsdp", None),
            P(None, None, "fsdp", None),
            P(None, None, "fsdp", None),
            P(None, "fsdp", None),
            P(None, "fsdp", None),
            P(None, "fsdp", None),
            P(None, None, None, "fsdp"),
            P(None, None, None, "fsdp"),
            P(None, None, None, "fsdp"),
            P("fsdp", None),
            P("fsdp", None),
            P("fsdp", None),
        ),
        check_vma=False,
    )
```

profile of v0, /device:TPU:0, one launch (start us, length us, event | category | flops | bytes accessed | tf_op | source)
XLA Modules:
  0.0 908.2 jit_solution(13257705563087266378)
XLA Ops:
  10.7 6.0 all-gather.12
  17.5 5.5 all_gather.57
  24.6 5.4 all-gather.1
  30.1 7.9 slice_reduce_fusion.19
  41.3 6.0 all-gather.2
  47.3 5.8 all-gather.3
  55.0 6.8 all-gather
  76.6 12.7 %copy.145 = bf16[2,3072,768]{2,1,0:T(8,128)(2,1)} copy(bf16[2,3072,768]{1,2,0:T(8,128)(2,1)} %pad_maximum_fusion) | data formatting | bytes 18874368 | tf_op jit(solution)/shard_map/concatenate | solution.py:87
  89.3 9.0 multiply_convert_fusion.5
  101.9 4.8 multiply_add_fusion.2
  106.7 6.6 copy.147
  113.3 9.4 %fusion.151 = (bf16[2,3072,256]{1,2,0:T(8,128)(2,1)S(1)}, f32[2,3072,256]{1,2,0:T(8,128)}) fusion(f32[2,3072,256]{1,2,0:T(8,128)} %get-tuple-element.144, f32[2,3072,256]{1,2,0:T(8,128)} %copy.147), kind=kLoop, calls=%fused_computation.353 | loop fusion | flops 3145728 | bytes 22020096 | tf_op jit(solution)/shard_map/convert_element_type | solution.py:23
  139.9 5.4 all-gather.5
  145.5 7.6 slice_reduce_fusion.9
  153.0 5.8 all-gather.6
  158.9 5.8 all-gather.7
  164.7 7.0 all-gather.4
  176.0 12.7 %copy.155 = bf16[2,3072,768]{2,1,0:T(8,128)(2,1)} copy(bf16[2,3072,768]{1,2,0:T(8,128)(2,1)} %pad_maximum_fusion.1) | data formatting | bytes 18874368 | tf_op jit(solution)/shard_map/concatenate | solution.py:87
  188.7 9.0 multiply_convert_fusion.4
  201.3 4.8 multiply_add_fusion.1
  206.1 6.5 copy.156
  212.7 9.3 %fusion.150 = (bf16[2,3072,256]{1,2,0:T(8,128)(2,1)S(1)}, f32[2,3072,256]{1,2,0:T(8,128)}) fusion(f32[2,3072,256]{1,2,0:T(8,128)} %get-tuple-element.130, f32[2,3072,256]{1,2,0:T(8,128)} %copy.156), kind=kLoop, calls=%fused_computation.352 | loop fusion | flops 3145728 | bytes 22020096 | tf_op jit(solution)/shard_map/convert_element_type | solution.py:23
  236.4 5.5 fusion.50
  246.9 5.7 all_gather.71
  252.6 5.6 all-gather.9
  258.3 7.6 slice_reduce_fusion.1
  265.9 5.8 all-gather.10
  271.7 6.3 all-gather.11
  278.0 6.6 all-gather.8
  284.9 40.8 %all-reduce = (f32[6]{0:T(128)S(1)}, f32[]{:T(128)}) all-reduce(f32[6]{0:T(128)S(1)} %reduce_sum.496, f32[]{:T(128)} %get-tuple-element.121), channel_id=1, replica_groups=mesh['dp'=8,'fsdp'=4] {'dp','fsdp'}, use_global_device_ids=true, to_apply=%region_14.15 | all-reduce | flops 7 | bytes 56 | tf_op jit(solution)/shard_map/psum | solution.py:203
  327.7 40.6 %psum.135 = f32[6]{0:T(128)S(1)} all-reduce(f32[6]{0:T(128)S(1)} %reduce_sum.500), channel_id=1, replica_groups=mesh['dp'=8,'fsdp'=4] {'dp','fsdp'}, use_global_device_ids=true, to_apply=%region_19.20 | all-reduce | flops 6 | bytes 48 | tf_op jit(solution)/shard_map/psum | solution.py:208
  368.9 9.2 %pad_maximum_fusion.2 = bf16[2,3072,768]{1,2,0:T(8,128)(2,1)} fusion(bf16[2,3072,256]{1,2,0:T(8,128)(2,1)} %copy-done.15, bf16[2,3072,256]{1,2,0:T(8,128)(2,1)} %fusion.50, bf16[2,3072,256]{1,2,0:T(8,128)(2,1)} %fusion.53), kind=kLoop, calls=%fused_computation.22 | loop fusion | flops 28311552 | bytes 18874368 | tf_op jit(solution)/shard_map/concatenate | solution.py:87
  378.2 12.6 %copy.164 = bf16[2,3072,768]{2,1,0:T(8,128)(2,1)} copy(bf16[2,3072,768]{1,2,0:T(8,128)(2,1)} %pad_maximum_fusion.2) | data formatting | bytes 18874368 | tf_op jit(solution)/shard_map/concatenate | solution.py:87
  390.8 9.0 multiply_convert_fusion.3
  403.4 4.9 multiply_add_fusion
  408.3 6.6 copy.165
  414.9 7.3 fusion.89
  441.4 5.0 fusion.29
  446.4 5.2 convert_reduce_fusion
  454.3 6.8 convert_reduce_fusion.1
  464.9 5.8 copy-done.4
  483.0 9.4 %fusion.138 = (f32[256]{0:T(256)}, f32[2,3072]{1,0:T(2,128)S(1)}, f32[2,3072,256]{2,1,0:T(8,128)S(1)}) fusion(f32[256]{0:T(256)S(1)} %copy-done.128, f32[2,512,512]{2,1,0:T(8,128)S(1)} %bitcast.340, s32[2,3072]{1,0:T(2,128)S(1)} %copy-done.90, f32[2,3072,256]{2,1,0:T(8,128)} %copy-done.8, f32[2,3072,768]{2,1,0:T(8,128)} %bitcast.324), kind=kOutput, calls=%fused_computation.347 | convolution fusion | flops 1621616384 | bytes 19449856 | tf_op jit(solution)/shard_map/sen,snd->sed/dot_general | solution.py:33
  492.4 5.0 fusion.28
  497.5 5.3 convert_reduce_fusion.2
  505.3 7.0 convert_reduce_fusion.3
  516.0 6.0 copy-done.5
  533.6 9.6 %fusion.139 = (f32[256]{0:T(256)}, f32[2,3072]{1,0:T(2,128)S(1)}, f32[2,3072,256]{2,1,0:T(8,128)S(1)}) fusion(f32[256]{0:T(256)S(1)} %copy-done.126, f32[2,512,512]{2,1,0:T(8,128)S(1)} %bitcast.338, s32[2,3072]{1,0:T(2,128)S(1)} %copy-done.90, f32[2,3072,256]{2,1,0:T(8,128)} %copy-done.6, f32[2,3072,768]{2,1,0:T(8,128)} %bitcast.326), kind=kOutput, calls=%fused_computation.348 | convolution fusion | flops 1621616384 | bytes 19449856 | tf_op jit(solution)/shard_map/sen,snd->sed/dot_general | solution.py:33
  543.3 5.0 fusion.27
  548.3 4.7 convert_reduce_fusion.4
  556.3 7.3 fusion.167
  563.6 8.4 fusion.166
  572.1 6.5 convert_reduce_fusion.5
  588.5 6.4 copy-done.3
  604.8 8.1 convert.50
  618.3 12.9 %reduce-scatter.28.cloned.1.call-done = f32[192,256]{1,0:T(8,128)} async-done(((f32[768,256]{1,0:T(8,128)}), f32[192,256]{1,0:T(8,128)}) %reduce-scatter.28.cloned.1.call-update) | async-done | bytes 196624 | tf_op jit(solution)/shard_map/reduce_scatter | solution.py:266
  631.1 25.9 %reduce-scatter.26.cloned.1.call-done = f32[192,256]{1,0:T(8,128)} async-done(((f32[768,256]{1,0:T(8,128)}), f32[192,256]{1,0:T(8,128)}) %reduce-scatter.26.cloned.1.call-update) | async-done | bytes 196624 | tf_op jit(solution)/shard_map/reduce_scatter | solution.py:266
  657.0 39.6 %psum.136 = f32[]{:T(128)} all-reduce(f32[]{:T(128)} %get-tuple-element.165), channel_id=1, replica_groups=mesh['dp'=8,'fsdp'=4] {'dp','fsdp'}, use_global_device_ids=true, to_apply=%region_21.22 | all-reduce | flops 1 | bytes 8 | tf_op jit(solution)/shard_map/psum | solution.py:247
  697.4 4.8 reduce-scatter.52.cloned.1.call-done
  703.1 21.7 %reduce-scatter.50.cloned.1.call-done = f32[64,8]{1,0:T(8,128)} async-done(((f32[256,8]{1,0:T(8,128)}), f32[64,8]{1,0:T(8,128)}) %reduce-scatter.50.cloned.1.call-update) | async-done | bytes 2064
  725.8 21.6 %reduce-scatter.48.cloned.1.call-done = f32[64,8]{1,0:T(8,128)} async-done(((f32[256,8]{1,0:T(8,128)}), f32[64,8]{1,0:T(8,128)}) %reduce-scatter.48.cloned.1.call-update) | async-done | bytes 2064
  748.4 21.7 %reduce-scatter.44.cloned.1.call-done = f32[64,78]{1,0:T(8,128)} async-done(((f32[256,78]{1,0:T(8,128)}), f32[64,78]{1,0:T(8,128)}) %reduce-scatter.44.cloned.1.call-update) | async-done | bytes 19984 | tf_op jit(solution)/shard_map/reduce_scatter | solution.py:287
  770.0 22.4 %reduce-scatter.24.cloned.1.call-done = f32[78,64]{0,1:T(8,128)} async-done(((f32[78,256]{0,1:T(8,128)}), f32[78,64]{0,1:T(8,128)}) %reduce-scatter.24.cloned.1.call-update) | async-done | bytes 19984 | tf_op jit(solution)/shard_map/reduce_scatter | solution.py:285
  792.5 40.0 %all-reduce.1 = (f32[78,64]{0,1:T(8,128)S(1)}, f32[4,64]{1,0:T(4,128)}, f32[1,2,4,64]{3,2,1,0:T(4,128)S(1)}, f32[1,2,4,64]{3,2,1,0:T(4,128)S(1)}, f32[1,2,4,64]{3,2,1,0:T(4,128)S(1)}, /*index=5*/f32[64,78]{1,0:T(8,128)S(1)}) all-reduce(f32[78,64]{0,1:T(8,128)} %reduce-scatter.24.cloned.1.call-done, ...), channel_id=1, replica_groups=mesh['dp'=8,'fsdp'=4] {'dp'}, use_global_device_ids=true, to_apply=%region_35.36 | all-reduce | flops 11776 | bytes 94208 | tf_op jit(solution)/shard_map/psum | solution.py:289
  838.1 48.7 %all-reduce.5.cloned.1.call-done = (f32[1,192,256]{2,1,0:T(8,128)}, f32[1,192,256]{2,1,0:T(8,128)}, f32[1,192,256]{2,1,0:T(8,128)}, f32[1,2,64,256]{3,2,1,0:T(8,...) async-done(((f32[1,192,256]{2,1,0:T(8,128)}, ...) | async-done | bytes 1376272 | tf_op jit(solution)/shard_map/psum | solution.py:271
  (586 shorter events, 183.9 us)
Async XLA Ops:
  7.2 54.6 %copy-start.58 = (f32[1024,78]{0,1:T(8,128)S(1)}, f32[1024,78]{0,1:T(8,128)}, u32[]{:S(2)}) copy-start(f32[1024,78]{0,1:T(8,128)} %param.30) | copy-start | bytes 958468
  7.2 54.6 %copy-start.60 = (f32[1024,78]{0,1:T(8,128)S(1)}, f32[1024,78]{0,1:T(8,128)}, u32[]{:S(2)}) copy-start(f32[1024,78]{0,1:T(8,128)} %param.29) | copy-start | bytes 958468
  7.2 55.6 %copy-start.90 = (s32[2,3072]{1,0:T(2,128)S(1)}, s32[2,3072]{1,0:T(2,128)}, u32[]{:S(2)}) copy-start(s32[2,3072]{1,0:T(2,128)} %param.34) | copy-start | bytes 73732
  7.2 610.9 %reduce-scatter.42.cloned.1.call-start = ((), (), s32[]{:S(2)}) async-start(), calls=%async_computation.24 | async-start | bytes 655360 | tf_op jit(solution)/shard_map/reduce_scatter | solution.py:268
  38.0 63.9 %copy-start.125 = (f32[256]{0:T(256)}, f32[256]{0:T(256)S(1)}, u32[]{:S(2)}) copy-start(f32[256]{0:T(256)S(1)} %get-tuple-element.68) | copy-start | bytes 3076
  38.0 92.8 %copy-start.130 = (f32[256]{0:T(256)}, f32[256]{0:T(256)S(1)}, u32[]{:S(2)}) copy-start(f32[256]{0:T(256)S(1)} %get-tuple-element.65) | copy-start | bytes 3076
  47.3 51.0 %copy-start.74 = (bf16[1,2,256,256]{3,2,1,0:T(8,128)(2,1)}, bf16[1,2,256,256]{3,2,1,0:T(8,128)(2,1)S(1)}, u32[]{:S(2)}) copy-start(bf16[1,2,256,256]{3,2,1,0:T(8,128)(2,1)S(1)} %all-gather.2) | copy-start | bytes 786436
  53.1 74.6 %copy-start.39 = (bf16[1,512,256]{2,1,0:T(8,128)(2,1)}, bf16[1,512,256]{2,1,0:T(8,128)(2,1)S(1)}, u32[]{:S(2)}) copy-start(bf16[1,512,256]{2,1,0:T(8,128)(2,1)S(1)} %all-gather.3) | copy-start | bytes 786436
  61.8 27.5 %copy-start.51 = (bf16[1,768,256]{2,1,0:T(8,128)(2,1)}, bf16[1,768,256]{2,1,0:T(8,128)(2,1)S(1)}, u32[]{:S(2)}) copy-start(bf16[1,768,256]{2,1,0:T(8,128)(2,1)S(1)} %all-gather) | copy-start | bytes 1179652
  130.3 102.4 %copy-start.9 = (f32[1024,256]{1,0:T(8,128)}, f32[1024,256]{1,0:T(8,128)S(1)}, u32[]{:S(2)}) copy-start(f32[1024,256]{1,0:T(8,128)S(1)} %get-tuple-element.152) | copy-start | bytes 3145732
  130.3 102.4 %copy-start.109 = (f32[1024]{0:T(1024)}, f32[1024]{0:T(1024)S(1)}, u32[]{:S(2)}) copy-start(f32[1024]{0:T(1024)S(1)} %broadcast_multiply_fusion.12) | copy-start | bytes 12292
  130.7 102.1 %copy-start.116 = (f32[1024]{0:T(1024)}, f32[1024]{0:T(1024)S(1)}, u32[]{:S(2)}) copy-start(f32[1024]{0:T(1024)S(1)} %add_rsqrt_fusion.5) | copy-start | bytes 12292
  137.1 15.9 %copy-start.106 = (bf16[1,2,64,256]{3,2,1,0:T(8,128)(2,1)S(1)}, bf16[1,2,64,256]{3,2,1,0:T(8,128)(2,1)}, u32[]{:S(2)}) copy-start(bf16[1,2,64,256]{3,2,1,0:T(8,128)(2,1)} %get-tuple-element.138) | copy-start | bytes 196612
  137.1 21.8 %copy-start.107 = (bf16[1,128,256]{2,1,0:T(8,128)(2,1)S(1)}, bf16[1,128,256]{2,1,0:T(8,128)(2,1)}, u32[]{:S(2)}) copy-start(bf16[1,128,256]{2,1,0:T(8,128)(2,1)} %get-tuple-element.135) | copy-start | bytes 196612
  137.1 34.6 %copy-start.17 = (bf16[2,3072,256]{1,2,0:T(8,128)(2,1)S(1)}, bf16[2,3072,256]{1,2,0:T(8,128)(2,1)}, u32[]{:S(2)}) copy-start(bf16[2,3072,256]{1,2,0:T(8,128)(2,1)} %copy-done.16) | copy-start | bytes 9437188
  153.0 48.3 %copy-start.127 = (f32[256]{0:T(256)}, f32[256]{0:T(256)S(1)}, u32[]{:S(2)}) copy-start(f32[256]{0:T(256)S(1)} %get-tuple-element.60) | copy-start | bytes 3076
  158.9 38.9 %copy-start.76 = (bf16[1,2,256,256]{3,2,1,0:T(8,128)(2,1)}, bf16[1,2,256,256]{3,2,1,0:T(8,128)(2,1)S(1)}, u32[]{:S(2)}) copy-start(bf16[1,2,256,256]{3,2,1,0:T(8,128)(2,1)S(1)} %all-gather.6) | copy-start | bytes 786436
  164.7 64.3 %copy-start.41 = (bf16[1,512,256]{2,1,0:T(8,128)(2,1)}, bf16[1,512,256]{2,1,0:T(8,128)(2,1)S(1)}, u32[]{:S(2)}) copy-start(bf16[1,512,256]{2,1,0:T(8,128)(2,1)S(1)} %all-gather.7) | copy-start | bytes 786436
  241.9 10.7 %copy-start.114 = (bf16[1,2,4,64]{2,1,0,3:T(2,128)(2,1)S(1)}, bf16[1,2,4,64]{2,1,0,3:T(2,128)(2,1)}, u32[]{:S(2)}) copy-start(bf16[1,2,4,64]{2,1,0,3:T(2,128)(2,1)} %get-tuple-element.140) | copy-start | bytes 3076
  241.9 23.9 %copy-start.104 = (bf16[1,2,64,256]{3,2,1,0:T(8,128)(2,1)S(1)}, bf16[1,2,64,256]{3,2,1,0:T(8,128)(2,1)}, u32[]{:S(2)}) copy-start(bf16[1,2,64,256]{3,2,1,0:T(8,128)(2,1)} %get-tuple-element.137) | copy-start | bytes 196612
  241.9 29.8 %copy-start.105 = (bf16[1,128,256]{2,1,0:T(8,128)(2,1)S(1)}, bf16[1,128,256]{2,1,0:T(8,128)(2,1)}, u32[]{:S(2)}) copy-start(bf16[1,128,256]{2,1,0:T(8,128)(2,1)} %get-tuple-element.134) | copy-start | bytes 196612
  241.9 36.1 %copy-start.91 = (bf16[1,192,256]{2,1,0:T(8,128)(2,1)S(1)}, bf16[1,192,256]{2,1,0:T(8,128)(2,1)}, u32[]{:S(2)}) copy-start(bf16[1,192,256]{2,1,0:T(8,128)(2,1)} %get-tuple-element.131) | copy-start | bytes 294916
  242.0 42.6 %copy-start.59 = (f32[1024,78]{0,1:T(8,128)S(1)}, f32[1024,78]{0,1:T(8,128)}, u32[]{:S(2)}) copy-start(f32[1024,78]{0,1:T(8,128)} %param.30) | copy-start | bytes 958468
  242.0 42.6 %copy-start.61 = (f32[1024,78]{0,1:T(8,128)S(1)}, f32[1024,78]{0,1:T(8,128)}, u32[]{:S(2)}) copy-start(f32[1024,78]{0,1:T(8,128)} %param.29) | copy-start | bytes 958468
  242.0 42.6 %copy-start.120 = (f32[1024]{0:T(1024)S(1)}, f32[1024]{0:T(1024)}, u32[]{:S(2)}) copy-start(f32[1024]{0:T(1024)} %and_select_fusion) | copy-start | bytes 12292
  271.7 128.1 %copy-start.79 = (bf16[1,2,256,256]{3,2,1,0:T(8,128)(2,1)}, bf16[1,2,256,256]{3,2,1,0:T(8,128)(2,1)S(1)}, u32[]{:S(2)}) copy-start(bf16[1,2,256,256]{3,2,1,0:T(8,128)(2,1)S(1)} %all-gather.10) | copy-start | bytes 786436
  284.6 106.2 %copy-start.54 = (bf16[1,768,256]{2,1,0:T(8,128)(2,1)}, bf16[1,768,256]{2,1,0:T(8,128)(2,1)S(1)}, u32[]{:S(2)}) copy-start(bf16[1,768,256]{2,1,0:T(8,128)(2,1)S(1)} %all-gather.8) | copy-start | bytes 1179652
  435.0 183.1 %reduce-scatter.36.cloned.1.call-start = ((), (), s32[]{:S(2)}) async-start(), calls=%async_computation.21 | async-start | bytes 655360 | tf_op jit(solution)/shard_map/reduce_scatter | solution.py:267
  454.3 163.9 %reduce-scatter.40.cloned.1.call-start = ((), (), s32[]{:S(2)}) async-start(), calls=%async_computation.23 | async-start | bytes 655360 | tf_op jit(solution)/shard_map/reduce_scatter | solution.py:268
  480.1 12.3 %slice-start.2 = ((s8[6291456]{0:T(1024)(128)(4,1)}), s8[2097152]{0:T(1024)(128)(4,1)S(1)}, s32[]{:S(2)}) async-start(s8[6291456]{0:T(1024)(128)(4,1)} %bitcast.317), calls=%async_computation.33 | async-start | bytes 4194304
  481.3 136.8 %reduce-scatter.34.cloned.1.call-start = ((), (), s32[]{:S(2)}) async-start(), calls=%async_computation.20 | async-start | bytes 655360 | tf_op jit(solution)/shard_map/reduce_scatter | solution.py:267
  505.2 113.0 %reduce-scatter.38.cloned.1.call-start = ((), (), s32[]{:S(2)}) async-start(), calls=%async_computation.22 | async-start | bytes 655360 | tf_op jit(solution)/shard_map/reduce_scatter | solution.py:268
  528.7 14.5 %copy-start.85 = (bf16[1024,256]{1,0:T(8,128)(2,1)}, bf16[1024,256]{1,0:T(8,128)(2,1)S(1)}, u32[]{:S(2)}) copy-start(bf16[1024,256]{1,0:T(8,128)(2,1)S(1)} %get-tuple-element.120) | copy-start | bytes 1572868
  530.6 12.6 %slice-start = ((s8[6291456]{0:T(1024)(128)(4,1)}), s8[2097152]{0:T(1024)(128)(4,1)S(1)}, s32[]{:S(2)}) async-start(s8[6291456]{0:T(1024)(128)(4,1)} %bitcast.315), calls=%async_computation.31 | async-start | bytes 4194304
  531.9 86.3 %reduce-scatter.32.cloned.1.call-start = ((), (), s32[]{:S(2)}) async-start(), calls=%async_computation.19 | async-start | bytes 655360 | tf_op jit(solution)/shard_map/reduce_scatter | solution.py:267
  533.5 9.7 %copy-start.24 = (f32[1024,512]{1,0:T(8,128)}, f32[1024,512]{1,0:T(8,128)S(1)}, u32[]{:S(2)}) copy-start(f32[1024,512]{1,0:T(8,128)S(1)} %fusion.121) | copy-start | bytes 6291460
  533.5 9.7 %slice-start.1 = ((s8[6291456]{0:T(1024)(128)(4,1)}), s8[4194304]{0:T(1024)(128)(4,1)S(1)}, s32[]{:S(2)}) async-start(s8[6291456]{0:T(1024)(128)(4,1)} %bitcast.315), calls=%async_computation.32 | async-start | bytes 8388608
  533.5 9.7 %copy-start.73 = (f32[6144]{0:T(1024)S(1)}, f32[6144]{0:T(1024)}, u32[]{:S(2)}) copy-start(f32[6144]{0:T(1024)} %copy-done.72) | copy-start | bytes 73732
  533.5 9.7 %copy-start.97 = (f32[6144]{0:T(1024)S(1)}, f32[6144]{0:T(1024)}, u32[]{:S(2)}) copy-start(f32[6144]{0:T(1024)} %copy-done.96) | copy-start | bytes 73732
  555.6 62.7 %reduce-scatter.30.cloned.1.call-start = ((), (), s32[]{:S(2)}) async-start(), calls=%async_computation.18 | async-start | bytes 983040 | tf_op jit(solution)/shard_map/reduce_scatter | solution.py:266
  563.6 67.6 %reduce-scatter.28.cloned.1.call-start = ((), (), s32[]{:S(2)}) async-start(), calls=%async_computation.17 | async-start | bytes 983040 | tf_op jit(solution)/shard_map/reduce_scatter | solution.py:266
  563.6 16.6 %slice-start.6 = ((s8[9437184]{0:T(1024)(128)(4,1)}), s8[1048576]{0:T(1024)(128)(4,1)S(1)}, s32[]{:S(2)}) async-start(s8[9437184]{0:T(1024)(128)(4,1)} %bitcast.328), calls=%async_computation.37 | async-start | bytes 2097152
  572.0 85.0 %reduce-scatter.26.cloned.1.call-start = ((), (), s32[]{:S(2)}) async-start(), calls=%async_computation.16 | async-start | bytes 983040 | tf_op jit(solution)/shard_map/reduce_scatter | solution.py:266
  583.8 11.1 %copy-start.95 = (f32[2,3072,4]{1,2,0:T(4,128)S(1)}, f32[2,3072,4]{1,2,0:T(4,128)}, u32[]{:S(2)}) copy-start(f32[2,3072,4]{1,2,0:T(4,128)} %param.35) | copy-start | bytes 294916
  583.9 112.7 %reduce-scatter.46.cloned.1.call-start = ((), (), s32[]{:S(2)}) async-start(), calls=%async_computation.26 | async-start | bytes 163840
  599.9 102.3 %reduce-scatter.52.cloned.1.call-start = ((), (), s32[]{:S(2)}) async-start(), calls=%async_computation.29 | async-start | bytes 163840
  601.1 123.7 %reduce-scatter.50.cloned.1.call-start = ((), (), s32[]{:S(2)}) async-start(), calls=%async_computation.28 | async-start | bytes 163840
  602.3 145.1 %reduce-scatter.48.cloned.1.call-start = ((), (), s32[]{:S(2)}) async-start(), calls=%async_computation.27 | async-start | bytes 163840
  603.5 166.5 %reduce-scatter.44.cloned.1.call-start = ((), (), s32[]{:S(2)}) async-start(), calls=%async_computation.25 | async-start | bytes 163840 | tf_op jit(solution)/shard_map/reduce_scatter | solution.py:287
  604.7 187.7 %reduce-scatter.24.cloned.1.call-start = ((), (), s32[]{:S(2)}) async-start(), calls=%async_computation.15 | async-start | bytes 163840 | tf_op jit(solution)/shard_map/reduce_scatter | solution.py:285
  614.9 217.7 %copy-start.138 = (f32[4,64]{1,0:T(4,128)S(1)}, f32[4,64]{1,0:T(4,128)}, u32[]{:S(2)}) copy-start(f32[4,64]{1,0:T(4,128)} %param.38) | copy-start | bytes 3076
  614.9 217.7 %copy-start.152 = (f32[4,64]{1,0:T(4,128)S(1)}, f32[4,64]{1,0:T(4,128)}, u32[]{:S(2)}) copy-start(f32[4,64]{1,0:T(4,128)} %param.52) | copy-start | bytes 3076
  614.9 219.0 %copy-start.124 = (f32[3,2,4,64]{3,2,1,0:T(4,128)S(1)}, f32[3,2,4,64]{3,2,1,0:T(4,128)}, u32[]{:S(2)}) copy-start(f32[3,2,4,64]{3,2,1,0:T(4,128)} %param.42) | copy-start | bytes 18436
  614.9 220.3 %copy-start.111 = (f32[78,64]{0,1:T(8,128)S(1)}, f32[78,64]{0,1:T(8,128)}, u32[]{:S(2)}) copy-start(f32[78,64]{0,1:T(8,128)} %param.37) | copy-start | bytes 59908
  614.9 220.3 %copy-start.129 = (f32[78,64]{0,1:T(8,128)S(1)}, f32[78,64]{0,1:T(8,128)}, u32[]{:S(2)}) copy-start(f32[78,64]{0,1:T(8,128)} %param.51) | copy-start | bytes 59908
  614.9 221.7 %copy-start.113 = (f32[64,78]{1,0:T(8,128)S(1)}, f32[64,78]{1,0:T(8,128)}, u32[]{:S(2)}) copy-start(f32[64,78]{1,0:T(8,128)} %param.43) | copy-start | bytes 59908
  614.9 280.1 %copy-start.49 = (f32[3,128,256]{2,1,0:T(8,128)S(1)}, f32[3,128,256]{2,1,0:T(8,128)}, u32[]{:S(2)}) copy-start(f32[3,128,256]{2,1,0:T(8,128)} %param.41) | copy-start | bytes 1179652
  615.0 280.1 %copy-start.92 = (f32[3,128,256]{2,1,0:T(8,128)S(1)}, f32[3,128,256]{2,1,0:T(8,128)}, u32[]{:S(2)}) copy-start(f32[3,128,256]{2,1,0:T(8,128)} %param.55) | copy-start | bytes 1179652
  615.0 280.1 %copy-start.93 = (f32[3,128,256]{2,1,0:T(8,128)S(1)}, f32[3,128,256]{2,1,0:T(8,128)}, u32[]{:S(2)}) copy-start(f32[3,128,256]{2,1,0:T(8,128)} %param.48) | copy-start | bytes 1179652
  616.9 279.4 %copy-start.50 = (f32[3,2,64,256]{3,2,1,0:T(8,128)S(1)}, f32[3,2,64,256]{3,2,1,0:T(8,128)}, u32[]{:S(2)}) copy-start(f32[3,2,64,256]{3,2,1,0:T(8,128)} %param.40) | copy-start | bytes 1179652
  617.0 281.7 %copy-start.38 = (f32[3,192,256]{2,1,0:T(8,128)S(1)}, f32[3,192,256]{2,1,0:T(8,128)}, u32[]{:S(2)}) copy-start(f32[3,192,256]{2,1,0:T(8,128)} %param.39) | copy-start | bytes 1769476
  617.0 281.6 %copy-start.81 = (f32[3,192,256]{2,1,0:T(8,128)S(1)}, f32[3,192,256]{2,1,0:T(8,128)}, u32[]{:S(2)}) copy-start(f32[3,192,256]{2,1,0:T(8,128)} %param.53) | copy-start | bytes 1769476
  617.0 281.6 %copy-start.82 = (f32[3,192,256]{2,1,0:T(8,128)S(1)}, f32[3,192,256]{2,1,0:T(8,128)}, u32[]{:S(2)}) copy-start(f32[3,192,256]{2,1,0:T(8,128)} %param.46) | copy-start | bytes 1769476
  618.0 268.7 %all-reduce.5.cloned.1.call-start = ((), (), s32[]{:S(2)}) async-start(), calls=%async_computation.30 | async-start | bytes 2752512 | tf_op jit(solution)/shard_map/psum | solution.py:271
  (133 other events, 657.0 us)
Sparse Core Ops, SparseCore 0:
  435.1 22.3 reduce-scatter.41
  460.1 21.6 reduce-scatter.35
  484.3 21.6 reduce-scatter.39
  508.5 21.6 reduce-scatter.33
  532.5 21.9 reduce-scatter.37
  557.6 21.6 reduce-scatter.31
  581.8 23.2 reduce-scatter.29
  607.8 23.2 reduce-scatter.27
  633.7 23.2 reduce-scatter.25
  660.0 19.5 reduce-scatter.45
  682.6 19.5 reduce-scatter.51
  705.2 19.5 reduce-scatter.49
  727.8 19.5 reduce-scatter.47
  750.4 19.5 reduce-scatter.43
  772.9 19.5 reduce-scatter.23
  797.6 89.0 all-reduce.4
where the time goes:
time: 917 us; the launch traced here: 908 us
  blocking collectives  251 us (27%)
  matrix products  188 us (21%)
  waiting for transfers between devices  180 us (20%)
  local copies, waits for them, and re-layouts  139 us (15%)
  other arithmetic  131 us (14%)
  between operations  19.5 us (2%)
    psum x1, waiting for transfers between devices, body(): lax.psum((owned_part[0], owned_part[1], owned_part[2], owned_part[3]), 'dp')  48.7 us
    unnamed x20, waiting for transfers between devices  48.4 us
    unnamed x391, local copies, waits for them, and re-layouts  45.9 us
    dot_general x9, matrix products, pick_rows(): jnp.einsum('sen,snd->sed', table, values, preferred_element_type=jnp.floa...  45.8 us
    psum x1, blocking collectives, body(): total_sum, total_count = lax.psum((local_sum, local_count), ('dp', 'fsdp'))  40.8 us
    psum x1, blocking collectives, body(): spread = lax.psum(jnp.sum(centered * centered, axis=(0, 2)), ('dp', 'fsdp'))  40.6 us
    psum x1, blocking collectives, body(): outer_grads = lax.psum((outer_part[0], outer_part[1], outer_part[2]), 'dp')  40 us
    psum x1, blocking collectives, body(): loss_sum = lax.psum(jnp.sum(weighting * misfit * misfit), ('dp', 'fsdp'))  39.6 us
  transfers between devices with their start and end apart: 16, of which 8 were waited for; matrix products, arithmetic and copies ran while one was open for 18% of the time, Pallas kernels for 0%

commit v1 on v0

v1 whole, which is shorter than its diff:
```python
import functools

import jax
import jax.numpy as jnp
from jax import lax
from jax.experimental import pallas as pl
from jax.experimental.pallas import tpu as pltpu
from jax.sharding import PartitionSpec as P

VARS = 6
LEVELS = 13
ROUNDS = 3
STEP = 10

norm_eps = 1e-05
stat_eps = 1e-06
beta_one = 0.9
beta_two = 0.999
adam_eps = 1e-08
decay_rate = 0.01
rate_matrix = 0.03
rate_vector = 0.2

BF = jnp.bfloat16
F32 = jnp.float32
VMEM_LIMIT = 56 * 1024 * 1024
EDGE_TILE = 512


def contract(a, b, da, db):
    return lax.dot_general(a, b, (((da,), (db,)), ((), ())), preferred_element_type=F32)


def nn(a, b):
    return contract(a, b, 1, 0)


def nt(a, b):
    return contract(a, b, 1, 1)


def tn(a, b):
    return contract(a, b, 0, 0)


def sigmoid(v):
    return 0.5 * jnp.tanh(0.5 * v) + 0.5


def round_up(v, m):
    return (v + m - 1) // m * m


class Plan:
    def __init__(self, latent, dp_size, fsdp_size):
        self.latent = latent
        self.dp = dp_size
        self.fsdp = fsdp_size
        self.width = latent // fsdp_size
        self.half = self.width // 2
        sizes = (
            ("edge_first", 3 * self.width),
            ("edge_second", self.width),
            ("node_second", self.width),
            ("node_first", 2 * self.width),
            ("rows", 16),
            ("outer", self.half),
        )
        offset = 0
        self.at = {}
        for name, size in sizes:
            self.at[name] = (offset, size)
            offset += size
        self.piece = round_up((offset + dp_size - 1) // dp_size, 16)
        self.used = offset
        self.total = self.piece * dp_size

    def pieces(self, name):
        start, size = self.at[name]
        done = 0
        while done < size:
            at = start + done
            count = min(size - done, self.piece - at % self.piece)
            yield at // self.piece, at % self.piece, done, count
            done += count


def params(**kw):
    return pltpu.CompilerParams(vmem_limit_bytes=VMEM_LIMIT, **kw)


def live_row(border, count):
    place = lax.broadcasted_iota(jnp.int32, border.shape, 1)
    return jnp.where((place < count) & (border != 1), 1.0, 0.0).astype(F32)


def group_matrix(rows, cols, flip):
    var = lax.broadcasted_iota(jnp.int32, (rows, cols), 1 if flip else 0)
    chan = lax.broadcasted_iota(jnp.int32, (rows, cols), 0 if flip else 1)
    inside = (chan >= var * LEVELS) & (chan < (var + 1) * LEVELS)
    return jnp.where(inside, 1.0, 0.0).astype(F32)


def exact(a, b):
    return lax.dot_general(
        a, b, (((1,), (0,)), ((), ())), precision=lax.Precision.HIGHEST, preferred_element_type=F32
    )


def pack_round(plan, out, r, edge_first, second_layers, node_first, vectors, edge_encoder, outer):
    width = plan.width
    at = plan.at

    def put(name, value):
        start, size = at[name]
        out[start : start + size, :] = value.astype(BF)

    put("edge_first", edge_first[r])
    put("edge_second", second_layers[r, 0])
    put("node_second", second_layers[r, 1])
    put("node_first", node_first[r])
    rows = jnp.concatenate([vectors[r, 0], vectors[r, 1]], axis=0)
    if edge_encoder is None:
        low = jnp.zeros((8, width), F32)
    else:
        low = jnp.concatenate([edge_encoder[...], jnp.zeros((4, width), F32)], axis=0)
    rows = jnp.concatenate([rows, low], axis=0)
    rows = jnp.concatenate([rows, jnp.zeros((16, plan.latent - width), F32)], axis=1)
    put("rows", rows)
    start, size = at["outer"]
    if outer is None:
        out[start : start + size, :] = jnp.zeros((size, plan.latent), BF)
    else:
        channels = outer.shape[1]
        wide = jnp.concatenate(
            [outer[...], jnp.zeros((width, plan.latent // 2 - channels), F32)], axis=1
        )
        put("outer", jnp.concatenate([wide[: plan.half], wide[plan.half :]], axis=1))
    if plan.total > plan.used:
        out[plan.used : plan.total, :] = jnp.zeros((plan.total - plan.used, plan.latent), BF)


def pack_first_kernel(plan, ef, sl, nf, vec, ee, enc, out):
    pack_round(plan, out, 0, ef, sl, nf, vec, ee, enc)


def pack_rest_kernel(plan, graphs, counts, ef, sl, nf, vec, dec, x_now, x_next, border, out1, out2, stats):
    pack_round(plan, out1, 1, ef, sl, nf, vec, None, None)
    pack_round(plan, out2, 2, ef, sl, nf, vec, None, dec)
    nodes = x_now.shape[1] // graphs
    channels = x_now.shape[0]
    lives = []
    for g in range(graphs):
        lives.append(live_row(border[:, g * nodes : (g + 1) * nodes], counts[g]))
    live = jnp.concatenate(lives, axis=1)
    delta = x_next[...] - x_now[...]
    count = jnp.sum(live)
    sums = jnp.sum(delta * live, axis=1, keepdims=True)
    to_var = group_matrix(8, channels, False)
    to_chan = group_matrix(channels, 8, True)
    var_sum = exact(to_var, jnp.broadcast_to(sums, (channels, 128)))
    mean = var_sum / (jnp.maximum(count, 1.0) * LEVELS)
    centered = (delta - exact(to_chan, mean)[:, 0:1]) * live
    square = jnp.sum(centered * centered, axis=1, keepdims=True)
    var_square = exact(to_var, jnp.broadcast_to(square, (channels, 128)))
    lane = lax.broadcasted_iota(jnp.int32, (8, 128), 1)
    value = jnp.where(lane == 0, var_sum, jnp.where(lane == 1, var_square, count))
    stats[...] = jnp.broadcast_to(value[None], stats.shape)


def assemble(plan, me, packs, edge_first, edge_second, node_second, node_first, cols, outer):
    width = plan.width
    latent = plan.latent
    total = jnp.zeros((latent, 16), F32)
    rowid = lax.broadcasted_iota(jnp.int32, (latent, width), 0)
    colid = lax.broadcasted_iota(jnp.int32, (latent, width), 1)
    for k, pack in enumerate(packs):
        owner = jnp.bitwise_xor(me, k)

        def put(ref, name, step):
            start, size = plan.at[name]
            ref[pl.ds(pl.multiple_of(owner * step, 16), size), :] = pack[start : start + size, :]

        put(edge_first, "edge_first", 3 * width)
        put(edge_second, "edge_second", width)
        put(node_second, "node_second", width)
        put(node_first, "node_first", 2 * width)
        start, size = plan.at["rows"]
        place = jnp.where(rowid == owner * width + colid, 1.0, 0.0).astype(BF)
        total = total + nt(place, pack[start : start + size, 0:width])
        if outer is not None:
            start, size = plan.at["outer"]
            half = latent // 2
            first = pl.multiple_of(owner * width, 16)
            second = pl.multiple_of(owner * width + plan.half, 16)
            outer[pl.ds(first, size), :] = pack[start : start + size, 0:half]
            outer[pl.ds(second, size), :] = pack[start : start + size, half : 2 * half]
    cols[...] = total


def fill_tables(u_ref, src, dst, nodes, tile):
    place = lax.broadcasted_iota(jnp.int32, (nodes, tile), 0).astype(jnp.int16)
    one = jnp.ones((nodes, tile), BF)
    zero = jnp.zeros((nodes, tile), BF)
    u_ref[0:nodes, :] = jnp.where(place == src.astype(jnp.int16), one, zero)
    u_ref[nodes : 2 * nodes, :] = jnp.where(place == dst.astype(jnp.int16), one, zero)


def norm_forward(z2, count):
    mean = jnp.sum(z2, axis=0, keepdims=True) * (1.0 / count)
    centered = z2 - mean
    var = jnp.sum(centered * centered, axis=0, keepdims=True) * (1.0 / count)
    inverse = lax.rsqrt(var + norm_eps)
    return centered * inverse, inverse


def forward_kernel(plan, first, last, graphs, tiles, me_ref, *refs):
    packs = refs[: plan.fsdp]
    refs = list(refs[plan.fsdp :])
    src_ref, dst_ref = refs[0:2]
    refs = refs[2:]
    if first:
        x_now, x_next, border, link = refs[0:4]
        refs = refs[4:]
    else:
        h_in, e_in = refs[0:2]
        refs = refs[2:]
    h_out, hb_out, agg_out, zn_out, xn_out, in_out, z1_out, xh_out, iv_out = refs[0:9]
    refs = refs[9:]
    if not last:
        e_out = refs[0]
        refs = refs[1:]
    wa, wb, wbn, wan, cols, outer, a_t, b_t, pcat, u, agg, h = refs[0:12]
    link8 = refs[12] if first else None
    latent = plan.latent
    nodes = h_out.shape[-1]
    tile = z1_out.shape[-1]
    g = pl.program_id(0)
    t = pl.program_id(1)

    @pl.when((g == 0) & (t == 0))
    def _():
        assemble(plan, me_ref[0], packs, wa, wb, wbn, wan, cols, outer if first else None)
        a_t[...] = wa[2 * latent :, :].astype(F32).T.astype(BF)
        b_t[...] = wb[...].astype(F32).T.astype(BF)
        pcat[:, 2 * nodes :] = a_t[...]
        if first:
            link8[...] = jnp.zeros_like(link8)

    @pl.when(t == 0)
    def _():
        if first:
            chosen = jnp.where(border[...] == 1, x_next[...], x_now[...]).astype(BF)
            h[...] = nn(outer[:, 0 : x_now.shape[0]], chosen)
        else:
            h[...] = h_in[0]
        low = h[...].astype(BF)
        hb_out[0] = low
        pcat[:, 0:nodes] = tn(wa[0:latent, :], low).astype(BF)
        pcat[:, nodes : 2 * nodes] = tn(wa[latent : 2 * latent, :], low).astype(BF)
        agg[...] = jnp.zeros_like(agg)

    fill_tables(u, src_ref[pl.ds(g, 1), :], dst_ref[pl.ds(g, 1), :], nodes, tile)
    if first:
        link8[0:4, :] = link[0]
        e = nn(cols[:, 8:16].astype(BF), link8[...].astype(BF))
    else:
        e = e_in[0]
    u[2 * nodes :, :] = e.astype(BF)
    z1 = nn(pcat[...], u[...]) + cols[:, 0:1]
    active = (z1 * sigmoid(z1)).astype(BF)
    z1_out[0] = z1.astype(BF)
    z2 = nn(b_t[...], active) + cols[:, 1:2]
    normed, inverse = norm_forward(z2, latent)
    xh_out[0] = normed.astype(BF)
    iv_out[0] = inverse
    e = e + (normed * cols[:, 2:3] + cols[:, 3:4])
    if not last:
        e_out[0] = e
    agg[...] += nt(e.astype(BF), u[nodes : 2 * nodes, :])

    @pl.when(t == tiles - 1)
    def _():
        arriving = agg[...].astype(BF)
        agg_out[0] = arriving
        low = h[...].astype(BF)
        z1n = tn(wan[0:latent, :], low) + tn(wan[latent:, :], arriving) + cols[:, 4:5]
        zn_out[0] = z1n
        actn = (z1n * sigmoid(z1n)).astype(BF)
        z2n = tn(wbn[...], actn) + cols[:, 5:6]
        normn, invn = norm_forward(z2n, latent)
        xn_out[0] = normn
        in_out[0] = invn
        h_out[0] = h[...] + (normn * cols[:, 6:7] + cols[:, 7:8])


def norm_backward(grad, gain, normed, inverse, count):
    scaled = grad * gain
    mean = jnp.sum(scaled, axis=0, keepdims=True) * (1.0 / count)
    cross = jnp.sum(scaled * normed, axis=0, keepdims=True) * (1.0 / count)
    return (inverse * (scaled - mean - normed * cross)).astype(BF)


def lane_sum(value):
    total = value[:, 0:128]
    for k in range(1, value.shape[1] // 128):
        total = total + value[:, 128 * k : 128 * (k + 1)]
    return total


def backward_kernel(plan, first, last, graphs, tiles, me_ref, counts, *refs):
    packs = refs[: plan.fsdp]
    refs = list(refs[plan.fsdp :])

    def take(k):
        out = refs[:k]
        del refs[:k]
        return out

    src_ref, dst_ref, hb, aggl, zn, xn, iv_n, z1_ref, xh_ref, iv_ref = take(10)
    if first:
        (link,) = take(1)
    else:
        (e_in,) = take(1)
    if last:
        h_fin, level, stats = take(3)
    else:
        gh_in, ge_in = take(2)
    if first or last:
        x_now, x_next, border = take(3)
    (out,) = take(1)
    if not first:
        gh_out, ge_out = take(2)
    if last:
        (count_out,) = take(1)
    wa, wb, wbn, wan, cols, outer = take(6)
    u, act, low_e, gh, gagg, q, d_ae, d_as, d_b, d_bn, d_an, v_e, v_n, loss = take(14)
    if first or last:
        d_outer, d_ee, link8, aux = take(4)
    latent = plan.latent
    nodes = hb.shape[-1]
    tile = z1_ref.shape[-1]
    channels = x_now.shape[0] if (first or last) else 0
    g = pl.program_id(0)
    t = pl.program_id(1)

    @pl.when((g == 0) & (t == 0))
    def _():
        assemble(plan, me_ref[0], packs, wa, wb, wbn, wan, cols, outer if (first or last) else None)
        for ref in (d_ae, d_as, d_b, d_bn, d_an, v_e, v_n, loss):
            ref[...] = jnp.zeros_like(ref)
        act[latent:, :] = jnp.ones((16, tile), BF)
        low_e[latent:, :] = jnp.ones((16, tile), BF)
        if first or last:
            d_outer[...] = jnp.zeros_like(d_outer)
            d_ee[...] = jnp.zeros_like(d_ee)
            link8[...] = jnp.zeros_like(link8)
        if last:
            total = jnp.sum(stats[...], axis=0)
            count = total[0:1, 2:3]
            mean = total[:, 0:1] / (count * LEVELS)
            spread = jnp.zeros((8, 1), F32)
            for k in range(stats.shape[0]):
                own = stats[k]
                own_count = own[:, 2:3]
                own_mean = own[:, 0:1] / (jnp.maximum(own_count, 1.0) * LEVELS)
                shift = own_mean - mean
                spread = spread + own[:, 1:2] + own_count * LEVELS * shift * shift
            variance = spread / (count * LEVELS)
            scale = jnp.broadcast_to(lax.rsqrt(variance + stat_eps), (8, 128))
            aux[:, 0:128] = exact(group_matrix(channels, 8, True), scale)
            aux[:, 128:256] = jnp.broadcast_to(count * channels, (channels, 128))
            count_out[0, 0] = jnp.sum(count) * channels

    @pl.when(t == 0)
    def _():
        if last:
            final_low = h_fin[0].astype(BF)
            delta = x_next[...] - x_now[...]
            scale = aux[:, 0:1]
            norm_count = aux[:, 128:129]
            predicted = tn(outer[...], final_low)[0:channels]
            misfit = (predicted - delta) * scale
            weighting = (level[...].astype(F32) + 1.0) / LEVELS * live_row(border[...], counts[g])
            piece = weighting * misfit * misfit
            loss[...] += jnp.broadcast_to(jnp.sum(piece), loss.shape)
            grad_pred = (2.0 * weighting * misfit * scale / norm_count).astype(BF)
            d_outer[:, 0:channels] += nt(final_low, grad_pred)
            gh_now = nn(outer[:, 0:channels], grad_pred)
        else:
            gh_now = gh_in[0]
        z1n = zn[0]
        normn = xn[0]
        v_n[:, 0:128] += lane_sum(gh_now * normn)
        v_n[:, 128:256] += lane_sum(gh_now)
        low_two = norm_backward(gh_now, cols[:, 6:7], normn, iv_n[0], latent)
        gate = sigmoid(z1n)
        soft = z1n * gate
        d_bn[0:latent] += nt(soft.astype(BF), low_two)
        d_active = nn(wbn[...], low_two)
        low_one = (d_active * (soft - soft * gate + gate)).astype(BF)
        v_n[:, 256:384] += lane_sum(low_one.astype(F32))
        v_n[:, 384:512] += lane_sum(low_two.astype(F32))
        low_h = hb[0]
        d_an[0:latent, :] += nt(low_h, low_one)
        d_an[latent:, :] += nt(aggl[0], low_one)
        gagg[...] = nn(wan[latent:, :], low_one).astype(BF)
        gh[...] = gh_now + nn(wan[0:latent, :], low_one)
        q[...] = jnp.zeros_like(q)

    fill_tables(u, src_ref[pl.ds(g, 1), :], dst_ref[pl.ds(g, 1), :], nodes, tile)
    if first:
        link8[0:4, :] = link[0]
        link_low = link8[...].astype(BF)
        low_e[0:latent, :] = nn(cols[:, 8:16].astype(BF), link_low).astype(BF)
    else:
        low_e[0:latent, :] = e_in[0].astype(BF)
    ge = nn(gagg[...], u[nodes : 2 * nodes, :])
    if not last:
        ge = ge + ge_in[0]
    normed = xh_ref[0].astype(F32)
    z1 = z1_ref[0].astype(F32)
    v_e[:, 0:128] += lane_sum(ge * normed)
    v_e[:, 128:256] += lane_sum(ge)
    low_two = norm_backward(ge, cols[:, 2:3], normed, iv_ref[0], latent)
    gate = sigmoid(z1)
    soft = z1 * gate
    act[0:latent, :] = soft.astype(BF)
    d_b[...] += nt(act[...], low_two)
    d_active = nn(wb[...], low_two)
    low_one = (d_active * (soft - soft * gate + gate)).astype(BF)
    d_ae[...] += nt(low_e[...], low_one)
    ge = ge + nn(wa[2 * latent :, :], low_one)
    q[...] += nt(low_one, u[...])
    if first:
        d_ee[...] += nt(ge.astype(BF), link_low)
    else:
        ge_out[0] = ge

    @pl.when(t == tiles - 1)
    def _():
        low_h = hb[0]
        total = gh[...]
        for side in range(2):
            sums = q[:, side * nodes : (side + 1) * nodes]
            high = sums.astype(BF)
            rest = (sums - high.astype(F32)).astype(BF)
            d_as[side * latent : (side + 1) * latent, :] += nt(low_h, high) + nt(low_h, rest)
            side_weights = wa[side * latent : (side + 1) * latent, :]
            total = total + nn(side_weights, high) + nn(side_weights, rest)
        if first:
            chosen = jnp.where(border[...] == 1, x_next[...], x_now[...]).astype(BF)
            d_outer[:, 0:channels] += nt(total.astype(BF), chosen)
        else:
            gh_out[0] = total

    @pl.when((g == graphs - 1) & (t == tiles - 1))
    def _():
        width = plan.width

        def emit(name, owner, value):
            for piece, row, at, count in plan.pieces(name):
                out[piece, owner, row : row + count, :] = value[at : at + count, :].astype(BF)

        def row_of(cols128):
            return jnp.sum(cols128.T, axis=0, keepdims=True)

        rows = [
            d_ae[latent : latent + 1, :],
            d_b[latent : latent + 1, :],
            row_of(v_e[:, 0:128]),
            row_of(v_e[:, 128:256]),
            row_of(v_n[:, 256:384]),
            row_of(v_n[:, 384:512]),
            row_of(v_n[:, 0:128]),
            row_of(v_n[:, 128:256]),
        ]
        top = jnp.concatenate(rows, axis=0)
        if first:
            low = d_ee[...].T
        else:
            whole = loss[0:1, 0:1]
            high = whole.astype(BF).astype(F32)
            mid = (whole - high).astype(BF).astype(F32)
            rest = whole - high - mid
            lane = lax.broadcasted_iota(jnp.int32, (8, latent), 1) % width
            low = jnp.where(lane == 0, high, jnp.where(lane == 1, mid, jnp.where(lane == 2, rest, 0.0)))
        all_rows = jnp.concatenate([top, low], axis=0)
        out[...] = jnp.zeros_like(out)
        pad = jnp.zeros((16, latent - width), F32)
        for j in range(plan.fsdp):
            block = 3 * width * j
            pieces = []
            if block < 2 * latent:
                stop = min(2 * latent, block + 3 * width)
                pieces.append(d_as[block:stop, :])
            if block + 3 * width > 2 * latent:
                begin = max(block, 2 * latent)
                pieces.append(d_ae[begin - 2 * latent : block + 3 * width - 2 * latent, :])
            emit("edge_first", j, pieces[0] if len(pieces) == 1 else jnp.concatenate(pieces, axis=0))
            emit("edge_second", j, d_b[width * j : width * (j + 1), :])
            emit("node_second", j, d_bn[width * j : width * (j + 1), :])
            emit("node_first", j, d_an[2 * width * j : 2 * width * (j + 1), :])
            emit(
                "rows", j, jnp.concatenate([all_rows[:, width * j : width * (j + 1)], pad], axis=1)
            )
            if first or last:
                own = d_outer[width * j : width * (j + 1), :]
                emit("outer", j, jnp.concatenate([own[: plan.half], own[plan.half :]], axis=1))


def adam_math(weight, moment, square, gradient, rate):
    moment_new = beta_one * moment + (1.0 - beta_one) * gradient
    square_new = beta_two * square + (1.0 - beta_two) * gradient * gradient
    direction = (
        moment_new
        * (1.0 / (1.0 - beta_one**STEP))
        / (jnp.sqrt(square_new * (1.0 / (1.0 - beta_two**STEP))) + adam_eps)
    )
    return (moment_new, square_new, weight - rate * (direction + decay_rate * weight))


def adam_kernel(plan, grads, *refs):
    ins = [refs[7 * k : 7 * k + 7] for k in range(3)]
    outs = [refs[21 + 3 * k : 24 + 3 * k] for k in range(7)]
    loss = refs[42]
    r = pl.program_id(0)
    block = grads[0]
    width = plan.width

    def part(name):
        start, size = plan.at[name]
        return block[start : start + size, :]

    def apply(k, index, gradient, rate):
        new = adam_math(ins[0][k][index], ins[1][k][index], ins[2][k][index], gradient, rate)
        for ref, value in zip(outs[k], new):
            ref[index] = value

    apply(2, 0, part("edge_first"), rate_matrix)
    apply(3, (0, 0), part("edge_second"), rate_matrix)
    apply(3, (0, 1), part("node_second"), rate_matrix)
    apply(4, 0, part("node_first"), rate_matrix)
    rows = part("rows")
    apply(5, (0, 0), rows[0:4, 0:width], rate_vector)
    apply(5, (0, 1), rows[4:8, 0:width], rate_vector)
    half = plan.latent // 2
    wide = part("outer")
    outer = jnp.concatenate([wide[:, 0:half], wide[:, half:]], axis=0)

    @pl.when(r == 0)
    def _():
        apply(0, Ellipsis, outer[:, 0 : ins[0][0].shape[1]], rate_matrix)
        apply(1, Ellipsis, rows[8:12, 0:width], rate_matrix)

    @pl.when(r == ROUNDS - 1)
    def _():
        apply(6, Ellipsis, outer[:, 0 : ins[0][6].shape[1]], rate_matrix)
        loss[0, 0] = jnp.sum(rows[8:9, 0:3])


def body(plan, *args):
    x_now, x_next, node_counts, border_flag, source_vertex, target_vertex, link_features, level_ids = args[:8]
    weights = args[8:15]
    moments = args[15:22]
    squares = args[22:29]
    encoder, edge_encoder, edge_first, second_layers, node_first, vectors, decoder = weights
    graphs, edge_count = source_vertex.shape
    nodes = x_now.shape[0] // graphs
    channels = x_now.shape[1]
    latent = plan.latent
    tile = EDGE_TILE
    tiles = edge_count // tile
    x_now_t = x_now.T
    x_next_t = x_next.T
    border = border_flag.reshape(1, -1)
    link_t = jnp.transpose(link_features, (0, 2, 1))
    level = level_ids.reshape(-1, 1)
    me = lax.axis_index("fsdp").astype(jnp.int32).reshape(1)
    devices = plan.dp * plan.fsdp

    vm = pl.BlockSpec(memory_space=pltpu.VMEM)
    sm = pl.BlockSpec(memory_space=pltpu.SMEM)
    sds = jax.ShapeDtypeStruct
    pack_shape = sds((plan.total, latent), BF)

    pack0 = pl.pallas_call(
        functools.partial(pack_first_kernel, plan),
        out_shape=pack_shape,
        in_specs=[vm] * 6,
        out_specs=vm,
        compiler_params=params(),
        name="pack_first",
    )(edge_first, second_layers, node_first, vectors, edge_encoder, encoder.T)

    def swap(value, mask):
        pairs = [(j, j ^ mask) for j in range(plan.fsdp)]
        return lax.ppermute(value, "fsdp", pairs)

    def spread_chain(own):
        got = [own]
        for k in range(1, plan.fsdp):
            low = k & -k
            got.append(swap(got[k & (k - 1)], low))
        return got

    def spread_direct(own):
        return [own] + [swap(own, k) for k in range(1, plan.fsdp)]

    packs = [spread_chain(pack0)]
    pack1, pack2, stats = pl.pallas_call(
        functools.partial(pack_rest_kernel, plan, graphs),
        out_shape=(pack_shape, pack_shape, sds((devices, 8, 128), F32)),
        in_specs=[sm] + [vm] * 8,
        out_specs=(vm,) * 3,
        compiler_params=params(),
        name="pack_rest",
    )(node_counts, edge_first, second_layers, node_first, vectors, decoder, x_now_t, x_next_t, border)
    packs.append(spread_direct(pack1))
    packs.append(spread_direct(pack2))
    stats = lax.all_to_all(stats, ("dp", "fsdp"), 0, 0, tiled=True)

    def const(shape):
        return pl.BlockSpec(shape, lambda g, t, *_: (0,) * len(shape))

    pack_spec = const((plan.total, latent))
    ids_spec = pl.BlockSpec((graphs, tile), lambda g, t, *_: (0, t))
    x_spec = pl.BlockSpec((channels, nodes), lambda g, t, *_: (0, g))
    border_spec = pl.BlockSpec((1, nodes), lambda g, t, *_: (0, g))
    link_spec = pl.BlockSpec((1, 4, tile), lambda g, t, *_: (g, 0, t))
    node_spec = pl.BlockSpec((1, latent, nodes), lambda g, t, *_: (g, 0, 0))
    node_row = pl.BlockSpec((1, 1, nodes), lambda g, t, *_: (g, 0, 0))
    edge_spec = pl.BlockSpec((1, latent, tile), lambda g, t, *_: (g * tiles + t, 0, 0))
    edge_row = pl.BlockSpec((1, 1, tile), lambda g, t, *_: (g * tiles + t, 0, 0))

    node_f32 = sds((graphs, latent, nodes), F32)
    node_bf = sds((graphs, latent, nodes), BF)
    node_row_f32 = sds((graphs, 1, nodes), F32)
    edge_f32 = sds((graphs * tiles, latent, tile), F32)
    edge_bf = sds((graphs * tiles, latent, tile), BF)
    edge_row_f32 = sds((graphs * tiles, 1, tile), F32)

    weight_scratch = [
        pltpu.VMEM((3 * latent, latent), BF),
        pltpu.VMEM((latent, latent), BF),
        pltpu.VMEM((latent, latent), BF),
        pltpu.VMEM((2 * latent, latent), BF),
        pltpu.VMEM((latent, 16), F32),
        pltpu.VMEM((latent, latent // 2), BF),
    ]
    row_flops = 2 * latent * latent
    forward_cost = pl.CostEstimate(
        flops=graphs * edge_count * row_flops * 8, bytes_accessed=24_000_000, transcendentals=0
    )
    backward_cost = pl.CostEstimate(
        flops=graphs * edge_count * row_flops * 11, bytes_accessed=30_000_000, transcendentals=0
    )

    stored = []
    state = None
    edge_state = None
    for r in range(ROUNDS):
        first = r == 0
        last = r == ROUNDS - 1
        ins = [*packs[r], source_vertex, target_vertex]
        specs = [pack_spec] * plan.fsdp + [ids_spec, ids_spec]
        if first:
            ins += [x_now_t, x_next_t, border, link_t]
            specs += [x_spec, x_spec, border_spec, link_spec]
        else:
            ins += [state, edge_state]
            specs += [node_spec, edge_spec]
        outs = [node_f32, node_bf, node_bf, node_f32, node_f32, node_row_f32, edge_bf, edge_bf, edge_row_f32]
        out_specs = [node_spec] * 5 + [node_row, edge_spec, edge_spec, edge_row]
        if not last:
            outs.append(edge_f32)
            out_specs.append(edge_spec)
        scratch = weight_scratch + [
            pltpu.VMEM((latent, latent), BF),
            pltpu.VMEM((latent, latent), BF),
            pltpu.VMEM((latent, 2 * nodes + latent), BF),
            pltpu.VMEM((2 * nodes + latent, tile), BF),
            pltpu.VMEM((latent, nodes), F32),
            pltpu.VMEM((latent, nodes), F32),
        ]
        if first:
            scratch = scratch + [pltpu.VMEM((8, tile), F32)]
        result = pl.pallas_call(
            functools.partial(forward_kernel, plan, first, last, graphs, tiles),
            out_shape=outs,
            grid_spec=pltpu.PrefetchScalarGridSpec(
                num_scalar_prefetch=1,
                grid=(graphs, tiles),
                in_specs=specs,
                out_specs=out_specs,
                scratch_shapes=scratch,
            ),
            compiler_params=params(),
            cost_estimate=forward_cost,
            name=f"forward_round{r}",
        )(me, *ins)
        stored.append((*result[1:9], edge_state))
        state = result[0]
        if not last:
            edge_state = result[9]

    blocks = [None] * ROUNDS
    loss_count = None
    grad_state = None
    grad_edge = None
    for r in reversed(range(ROUNDS)):
        first = r == 0
        last = r == ROUNDS - 1
        hb, aggl, zn, xn, ivn, z1, xh, iv, e_in = stored[r]
        ins = [*packs[r], source_vertex, target_vertex, hb, aggl, zn, xn, ivn, z1, xh, iv]
        specs = [pack_spec] * plan.fsdp + [ids_spec, ids_spec] + [node_spec] * 4
        specs += [node_row, edge_spec, edge_spec, edge_row]
        if first:
            ins += [link_t]
            specs += [link_spec]
        else:
            ins += [e_in]
            specs += [edge_spec]
        if last:
            ins += [state, level, stats]
            specs += [node_spec, const((channels, 1)), const((devices, 8, 128))]
        else:
            ins += [grad_state, grad_edge]
            specs += [node_spec, edge_spec]
        if first or last:
            ins += [x_now_t, x_next_t, border]
            specs += [x_spec, x_spec, border_spec]
        out_block = (plan.dp, plan.fsdp, plan.piece, latent)
        outs = [sds(out_block, BF)]
        out_specs = [const(out_block)]
        if not first:
            outs += [node_f32, edge_f32]
            out_specs += [node_spec, edge_spec]
        if last:
            outs += [sds((1, 1), F32)]
            out_specs += [sm]
        scratch = weight_scratch + [
            pltpu.VMEM((2 * nodes, tile), BF),
            pltpu.VMEM((latent + 16, tile), BF),
            pltpu.VMEM((latent + 16, tile), BF),
            pltpu.VMEM((latent, nodes), F32),
            pltpu.VMEM((latent, nodes), BF),
            pltpu.VMEM((latent, 2 * nodes), F32),
            pltpu.VMEM((latent + 16, latent), F32),
            pltpu.VMEM((2 * latent, latent), F32),
            pltpu.VMEM((latent + 16, latent), F32),
            pltpu.VMEM((latent, latent), F32),
            pltpu.VMEM((2 * latent, latent), F32),
            pltpu.VMEM((latent, 256), F32),
            pltpu.VMEM((latent, 512), F32),
            pltpu.VMEM((8, 128), F32),
        ]
        if first or last:
            scratch = scratch + [
                pltpu.VMEM((latent, latent // 2), F32),
                pltpu.VMEM((latent, 8), F32),
                pltpu.VMEM((8, tile), F32),
                pltpu.VMEM((channels, 256), F32),
            ]
        result = pl.pallas_call(
            functools.partial(backward_kernel, plan, first, last, graphs, tiles),
            out_shape=outs,
            grid_spec=pltpu.PrefetchScalarGridSpec(
                num_scalar_prefetch=2,
                grid=(graphs, tiles),
                in_specs=specs,
                out_specs=out_specs,
                scratch_shapes=scratch,
            ),
            compiler_params=params(),
            cost_estimate=backward_cost,
            name=f"backward_round{r}",
        )(me, node_counts, *ins)
        if not first:
            grad_state, grad_edge = result[1:3]
        if last:
            loss_count = result[3].reshape(())
        send = result[0].reshape(devices, plan.piece, latent)
        got = lax.all_to_all(send, ("dp", "fsdp"), 0, 0, tiled=True)
        total = jnp.sum(got.astype(F32), axis=0)
        shared = jnp.broadcast_to(total[None], (plan.dp, plan.piece, latent))
        whole = lax.all_to_all(shared, "dp", 0, 0, tiled=True)
        blocks[r] = whole.reshape(1, plan.total, latent)

    grads = jnp.concatenate(blocks, axis=0)

    def turned(group):
        return (group[0].T, *group[1:])

    groups = (turned(weights), turned(moments), turned(squares))

    def by_round(shape):
        if len(shape) == 2:
            return pl.BlockSpec(shape, lambda r: (0, 0))
        rest = (0,) * (len(shape) - 1)
        return pl.BlockSpec((1, *shape[1:]), lambda r: (r, *rest))

    shapes = [w.shape for w in groups[0]]
    each = [by_round(s) for s in shapes]
    out_specs = []
    out_shapes = []
    for s in shapes:
        out_specs += [by_round(s)] * 3
        out_shapes += [sds(s, F32)] * 3
    out_specs.append(sm)
    out_shapes.append(sds((1, 1), F32))
    new = pl.pallas_call(
        functools.partial(adam_kernel, plan),
        out_shape=out_shapes,
        grid=(ROUNDS,),
        in_specs=[pl.BlockSpec((1, plan.total, latent), lambda r: (r, 0, 0))] + each * 3,
        out_specs=out_specs,
        compiler_params=params(),
        name="update",
    )(grads, *groups[0], *groups[1], *groups[2])
    encoder_new = [v.T for v in new[0:3]]
    return (new[21].reshape(()), loss_count, *encoder_new, *new[3:21])


def solution(mesh):
    rows = P(("dp", "fsdp"), None)
    row = P(("dp", "fsdp"))
    weight_specs = (
        P(None, "fsdp"),
        P(None, "fsdp"),
        P(None, "fsdp", None),
        P(None, None, "fsdp", None),
        P(None, "fsdp", None),
        P(None, None, None, "fsdp"),
        P("fsdp", None),
    )
    placed = (rows, rows, row, row, rows, rows, P(("dp", "fsdp"), None, None), P(), *weight_specs * 3)
    out_specs = [P(), P()]
    for spec in weight_specs:
        out_specs += [spec] * 3

    def step(*args):
        plan = Plan(args[10].shape[2], mesh.shape["dp"], mesh.shape["fsdp"])
        return body(plan, *args)

    return jax.shard_map(
        step, mesh=mesh, in_specs=placed, out_specs=tuple(out_specs), check_vma=False
    )
```

time: 917 us -> 333 us (0.36)
  matrix products: 188 us -> 0 us
  blocking collectives: 251 us -> 79.2 us
  Pallas kernels: 0 us -> 159 us
  local copies, waits for them, and re-layouts: 139 us -> 5.04 us
  other arithmetic: 131 us -> 1.73 us
  waiting for transfers between devices: 180 us -> 61.7 us
  starting transfers between devices: 0.67 us -> 24.5 us
  between operations: 19.5 us -> 1.01 us
    dot_general x61 -> x0, matrix products: 188 us -> none  [the longest x9 45.8 us: pick_rows(): jnp.einsum('sen,snd->sed', table, values, preferred_element_type=jnp.floa...]
    psum x4 -> x0, blocking collectives: 161 us -> none  [the longest x1 40.8 us: body(): total_sum, total_count = lax.psum((local_sum, local_count), ('dp', 'fsdp'))]
    pallas_call x0 -> x9, Pallas kernels: none -> 159 us  [the longest x3 78.7 us: body(): pl.pallas_call(functools.partial(backward_kernel, plan, first, last, grap...]
    all_gather x15 -> x0, blocking collectives: 89.6 us -> none  [the longest x3 20.3 us: body(): lax.all_gather(to_low(edge_first[index_round]), 'fsdp', axis=0, tiled=True)]
    reduce_scatter x11 -> x0, waiting for transfers between devices: 83 us -> none  [the longest x3 38.8 us: body(): lax.psum_scatter(gradients[0], 'fsdp', scatter_dimension=0, tiled=True)]
    all_to_all x0 -> x3, blocking collectives: none -> 79.2 us  [the longest x2 61.1 us: body(): got = lax.all_to_all(send, ('dp', 'fsdp'), 0, 0, tiled=True)]
    all_to_all x0 -> x4, waiting for transfers between devices: none -> 55.2 us  [the longest x2 29.1 us: body(): whole = lax.all_to_all(shared, 'dp', 0, 0, tiled=True)]
    psum x1 -> x0, waiting for transfers between devices: 48.7 us -> none  [body(): lax.psum((owned_part[0], owned_part[1], owned_part[2], owned_part[3]), 'dp')]
  transfers between devices with their start and end apart: 16 -> 13, of which waited for: 8 -> 4; matrix products, arithmetic and copies ran while one was open for 18% -> 0% of each run, Pallas kernels for 0% -> 21%
where the time goes in v1:
time: 333 us; the launch traced here: 332 us
  Pallas kernels  159 us (48%)
  blocking collectives  79.2 us (24%)
  waiting for transfers between devices  61.7 us (19%)
  starting transfers between devices  24.5 us (7%)
  local copies, waits for them, and re-layouts  5.04 us (2%)
    pallas_call x3, Pallas kernels, body(): pl.pallas_call(functools.partial(backward_kernel, plan, first, last, grap...  78.7 us
    pallas_call x3, Pallas kernels, body(): pl.pallas_call(functools.partial(forward_kernel, plan, first, last, graph...  68.1 us
    all_to_all x2, blocking collectives, body(): got = lax.all_to_all(send, ('dp', 'fsdp'), 0, 0, tiled=True)  61.1 us
    all_to_all x2, waiting for transfers between devices, body(): whole = lax.all_to_all(shared, 'dp', 0, 0, tiled=True)  29.1 us
    all_to_all x1, waiting for transfers between devices, body(): got = lax.all_to_all(send, ('dp', 'fsdp'), 0, 0, tiled=True)  26.1 us
    all_to_all x1, blocking collectives, body(): whole = lax.all_to_all(shared, 'dp', 0, 0, tiled=True)  18.1 us
    ppermute x9, starting transfers between devices, swap(): return lax.ppermute(value, 'fsdp', pairs)  7.36 us
    all_to_all x2, starting transfers between devices, body(): whole = lax.all_to_all(shared, 'dp', 0, 0, tiled=True)  7.29 us
  transfers between devices with their start and end apart: 13, of which 4 were waited for; matrix products, arithmetic and copies ran while one was open for 0% of the time, Pallas kernels for 21%

profile of v1, /device:TPU:0, one launch (start us, length us, event | category | flops | bytes accessed | tf_op | source)
XLA Modules:
  0.0 331.7 jit_solution(3912235121139430686)
XLA Ops:
  0.7 0.0 copy-start.2
  0.7 2.0 pack_first.1.refs_0_
  2.7 3.0 collective-permute-start.1
  5.7 0.0 collective-permute-start
  5.7 6.5 %collective-permute-done.1.refs_2_ = bf16[512,256]{1,0:T(8,128)(2,1)S(1)} collective-permute-done((bf16[512,256]{1,0:T(8,128)(2,1)}, bf16[512,256]{1,0:T(8,128)(2,1)S(1)}, u32[]{:S(2)}, u32[]{:S(2)}) %collective-permute-start.1) | collective-permute-done | bytes 262176 | tf_op jit(solution)/shard_map/ppermute | solution.py:598
  12.2 0.0 collective-permute-start.2
  12.2 3.2 pack_rest.1
  15.4 1.8 collective-permute-start.5
  17.1 0.3 collective-permute-start.4
  17.4 0.0 collective-permute-start.3
  17.4 6.2 %all-to-all-start = ((f32[32,8,128]{2,1,0:T(8,128)}), f32[32,8,128]{2,1,0:T(8,128)S(1)}, u32[]{:S(2)}, u32[]{:S(2)}) async-start(f32[32,8,128]{2,1,0:T(8,128)} %get-tuple-element.115), calls=%async_computation | async-start | bytes 262144 | tf_op jit(solution)/shard_map/all_to_all | solution.py:621
  23.6 0.0 copy-done.2
  23.6 0.7 copy.52.refs_16_
  24.3 0.0 collective-permute-done.refs_1_
  24.3 1.5 collective-permute-start.8
  25.9 0.0 collective-permute-done.2.refs_3_
  25.9 0.4 collective-permute-start.7
  26.2 0.0 copy-done.3
  26.2 0.0 copy-done.4
  26.2 0.3 copy-done.5
  26.6 23.9 %forward_round0.1 = (f32[2,256,512]{2,1,0:T(8,128)}, bf16[2,256,512]{2,1,0:T(8,128)(2,1)}, bf16[2,256,512]{2,1,0:T(8,128)(2,1)}, f32[2,256,512]{2,1,0:T(8,128)},...) custom-call(s32[1]{0:T(128)} %bitcast.me_ref, ...), custom_call_target="tpu_custom_call" | custom-call | flops 6442450944 | bytes 24000000 | tf_op jit(solution)/shard_map/forward_round0/pallas_call | solution.py:688
  50.5 0.0 collective-permute-done.5.refs_3_
  50.5 0.0 copy-done.9
  50.5 0.0 copy-start.6
  50.6 0.4 collective-permute-start.6
  51.0 0.0 collective-permute-done.4.refs_2_
  51.0 0.0 collective-permute-done.3.refs_1_
  51.0 0.0 copy-start.8
  51.0 0.2 copy-done.6
  51.2 0.4 copy-done.7
  51.7 0.1 copy-done.8
  51.8 22.4 %forward_round1.1 = (f32[2,256,512]{2,1,0:T(8,128)}, bf16[2,256,512]{2,1,0:T(8,128)(2,1)}, bf16[2,256,512]{2,1,0:T(8,128)(2,1)}, f32[2,256,512]{2,1,0:T(8,128)},...) custom-call(s32[1]{0:T(128)} %bitcast.me_ref, ...), custom_call_target="tpu_custom_call" | custom-call | flops 6442450944 | bytes 24000000 | tf_op jit(solution)/shard_map/forward_round1/pallas_call | solution.py:688
  74.2 0.0 collective-permute-done.8.refs_3_
  74.2 0.0 copy-start.10
  74.2 0.0 collective-permute-done.7.refs_2_
  74.2 0.0 copy-start.11
  74.2 0.0 collective-permute-done.6.refs_1_
  74.2 0.0 copy-start.12
  74.2 0.6 copy-done.10
  74.9 0.1 copy-done.11
  75.0 0.1 copy-done.12
  75.0 21.8 %forward_round2.1 = (f32[2,256,512]{2,1,0:T(8,128)}, bf16[2,256,512]{2,1,0:T(8,128)(2,1)}, bf16[2,256,512]{2,1,0:T(8,128)(2,1)}, f32[2,256,512]{2,1,0:T(8,128)},...) custom-call(s32[1]{0:T(128)} %bitcast.me_ref, ...), custom_call_target="tpu_custom_call" | custom-call | flops 6442450944 | bytes 24000000 | tf_op jit(solution)/shard_map/forward_round2/pallas_call | solution.py:688
  96.8 0.0 all-to-all-done.refs_17_
  96.9 0.0 copy-start.1
  96.9 0.7 copy-done.1
  97.5 26.1 %backward_round2.1 = (bf16[8,4,64,256]{3,2,1,0:T(8,128)(2,1)}, f32[2,256,512]{2,1,0:T(8,128)}, f32[12,256,512]{2,1,0:T(8,128)}, f32[1,1]{1,0:T(1,128)}) custom-call(s32[1]{0:T(128)} %bitcast.me_ref, s32[2]{0:T(128)} %counts.7, bf16[512,256]{1,0:T(8,128)(2,1)} %get-tuple-element.103.refs_0_, bf16[512,256]{1,0:T(8,128)(2,1)} %copy-done.12, ...), custom_call_target="tpu_custom_call" | custom-call | flops 8858370048 | bytes 30000000 | tf_op jit(solution)/shard_map/backward_round2/pallas_call | solution.py:765
  123.7 25.6 %backward_round1.1 = (bf16[8,4,64,256]{3,2,1,0:T(8,128)(2,1)}, f32[2,256,512]{2,1,0:T(8,128)}, f32[12,256,512]{2,1,0:T(8,128)}) custom-call(s32[1]{0:T(128)} %bitcast.me_ref, s32[2]{0:T(128)} %counts.7, bf16[512,256]{1,0:T(8,128)(2,1)} %get-tuple-element.92.refs_0_, bf16[512,256]{1,0:T(8,128)(2,1)} %copy-done.8, bf16[512,256]{1,0:T(8,128)(2,1)} %copy-done.7, ...), custom_call_target="tpu_custom_call" | custom-call | flops 8858370048 | bytes 30000000 | tf_op jit(solution)/shard_map/backward_round1/pallas_call | solution.py:765
  149.3 27.0 %backward_round0.1 = bf16[8,4,64,256]{3,2,1,0:T(8,128)(2,1)} custom-call(s32[1]{0:T(128)} %bitcast.me_ref, s32[2]{0:T(128)} %counts.7, bf16[512,256]{1,0:T(8,128)(2,1)} %pack_first.1.refs_0_, bf16[512,256]{1,0:T(8,128)(2,1)} %copy-done.4, bf16[512,256]{1,0:T(8,128)(2,1)} %copy-done.3, bf16[512,256]{1,0:T(8,128)(2,1)} %copy-done.5, s32[2,3072]{1,0:T(2,128)} %refs_4_.12, ...), custom_call_target="tpu_custom_call" | custom-call | flops 8858370048 | bytes 30000000 | tf_op jit(solution)/shard_map/backward_round0/pallas_call | solution.py:765
  176.3 31.4 %all_to_all.35 = bf16[32,64,256]{2,1,0:T(8,128)(2,1)S(1)} all-to-all(bf16[32,64,256]{2,1,0:T(8,128)(2,1)} %bitcast.25), channel_id=1, replica_groups=mesh['dp'=8,'fsdp'=4] {'dp','fsdp'}, dimensions={0} | all-to-all | bytes 2097152 | tf_op jit(solution)/shard_map/all_to_all | solution.py:784
  207.7 29.7 %all_to_all.36 = bf16[32,64,256]{2,1,0:T(8,128)(2,1)S(1)} all-to-all(bf16[32,64,256]{2,1,0:T(8,128)(2,1)S(1)} %bitcast.23), channel_id=1, replica_groups=mesh['dp'=8,'fsdp'=4] {'dp','fsdp'}, dimensions={0} | all-to-all | bytes 2097152 | tf_op jit(solution)/shard_map/all_to_all | solution.py:784
  237.4 3.6 %all-to-all-start.3 = ((bf16[32,64,256]{2,1,0:T(8,128)(2,1)}), bf16[32,64,256]{2,1,0:T(8,128)(2,1)S(1)}, u32[]{:S(2)}, u32[]{:S(2)}) async-start(bf16[32,64,256]{2,1,0:T(8,128)(2,1)} %bitcast.24), calls=%async_computation.3 | async-start | bytes 2097152 | tf_op jit(solution)/shard_map/all_to_all | solution.py:784
  241.0 0.2 convert_reduce_fusion
  241.1 26.1 %all-to-all-done.3 = bf16[32,64,256]{2,1,0:T(8,128)(2,1)S(1)} async-done(((bf16[32,64,256]{2,1,0:T(8,128)(2,1)}), bf16[32,64,256]{2,1,0:T(8,128)(2,1)S(1)}, u32[]{:S(2)}, u32[]{:S(2)}) %all-to-all-start.3) | async-done | bytes 1048608 | tf_op jit(solution)/shard_map/all_to_all | solution.py:784
  267.2 0.8 broadcast_in_dim.8
  268.1 3.7 %all-to-all-start.6 = ((f32[8,64,256]{2,1,0:T(8,128)}), f32[8,64,256]{2,1,0:T(8,128)S(1)}, u32[]{:S(2)}, u32[]{:S(2)}) async-start(f32[8,64,256]{2,1,0:T(8,128)} %broadcast_in_dim.8), calls=%async_computation.6 | async-start | bytes 1048576 | tf_op jit(solution)/shard_map/all_to_all | solution.py:787
  271.7 0.2 convert_reduce_fusion.1
  271.9 14.6 %all-to-all-done.6 = f32[8,64,256]{2,1,0:T(8,128)S(1)} async-done(((f32[8,64,256]{2,1,0:T(8,128)}), f32[8,64,256]{2,1,0:T(8,128)S(1)}, u32[]{:S(2)}, u32[]{:S(2)}) %all-to-all-start.6) | async-done | bytes 524320 | tf_op jit(solution)/shard_map/all_to_all | solution.py:787
  286.4 0.8 broadcast_in_dim.7
  287.3 3.6 %all-to-all-start.4 = ((f32[8,64,256]{2,1,0:T(8,128)}), f32[8,64,256]{2,1,0:T(8,128)S(1)}, u32[]{:S(2)}, u32[]{:S(2)}) async-start(f32[8,64,256]{2,1,0:T(8,128)} %broadcast_in_dim.7), calls=%async_computation.4 | async-start | bytes 1048576 | tf_op jit(solution)/shard_map/all_to_all | solution.py:787
  290.9 0.2 convert_reduce_fusion.2
  291.1 14.5 %all-to-all-done.4 = f32[8,64,256]{2,1,0:T(8,128)S(1)} async-done(((f32[8,64,256]{2,1,0:T(8,128)}), f32[8,64,256]{2,1,0:T(8,128)S(1)}, u32[]{:S(2)}, u32[]{:S(2)}) %all-to-all-start.4) | async-done | bytes 524320 | tf_op jit(solution)/shard_map/all_to_all | solution.py:787
  305.6 18.1 %all_to_all.37 = f32[8,64,256]{2,1,0:T(8,128)S(1)} all-to-all(f32[8,64,256]{2,1,0:T(8,128)S(1)} %broadcast_in_dim.6), channel_id=1, replica_groups=mesh['dp'=8,'fsdp'=4] {'dp'}, dimensions={0} | all-to-all | bytes 1048576 | tf_op jit(solution)/shard_map/all_to_all | solution.py:787
  323.7 1.3 pad_maximum_fusion.grads
  325.0 6.5 %update.1 = (f32[64,78]{1,0:T(8,128)}, f32[64,78]{1,0:T(8,128)}, f32[64,78]{1,0:T(8,128)}, f32[4,64]{1,0:T(4,128)}, f32[4,64]{1,0:T(4,128)}, /*index=5*/f32[4,64...) custom-call(f32[3,512,256]{2,1,0:T(8,128)} %pad_maximum_fusion.grads, ...), custom_call_target="tpu_custom_call" | custom-call | tf_op jit(solution)/shard_map/update/pallas_call | solution.py:812
  (8 shorter events, 0.0 us)
Async XLA Ops:
  0.7 23.0 %copy-start.2 = (s32[78]{0:T(128)S(1)}, s32[78]{0:T(128)}, u32[]{:S(2)}) copy-start(s32[78]{0:T(128)} %param.36) | copy-start | bytes 940
  2.7 9.5 %collective-permute-start.1 = (bf16[512,256]{1,0:T(8,128)(2,1)}, bf16[512,256]{1,0:T(8,128)(2,1)S(1)}, u32[]{:S(2)}, u32[]{:S(2)}) collective-permute-start(bf16[512,256]{1,0:T(8,128)(2,1)} %pack_first.1.refs_0_), channel_id=1, source_target_pairs={{0,2},{1,3},{2,0},{3,1},{4,6},{5,7},{6,4},{7,5},{8,10},{9,11},{10,... | collective-permute-start | bytes 786440 | tf_op jit(solution)/shard_map/ppermute | solution.py:598
  5.7 18.7 %collective-permute-start = (bf16[512,256]{1,0:T(8,128)(2,1)}, bf16[512,256]{1,0:T(8,128)(2,1)S(1)}, u32[]{:S(2)}, u32[]{:S(2)}) collective-permute-start(bf16[512,256]{1,0:T(8,128)(2,1)} %pack_first.1.refs_0_), channel_id=1, source_target_pairs={{0,1},{1,0},{2,3},{3,2},{4,5},{5,4},{6,7},{7,6},{8,9},{9,8},{10,11... | collective-permute-start | bytes 786440 | tf_op jit(solution)/shard_map/ppermute | solution.py:598
  12.2 14.0 %copy-start.3 = (bf16[512,256]{1,0:T(8,128)(2,1)}, bf16[512,256]{1,0:T(8,128)(2,1)S(1)}, u32[]{:S(2)}) copy-start(bf16[512,256]{1,0:T(8,128)(2,1)S(1)} %collective-permute-done.1.refs_2_) | copy-start | bytes 786436
  12.2 13.7 %collective-permute-start.2 = (bf16[512,256]{1,0:T(8,128)(2,1)S(1)}, bf16[512,256]{1,0:T(8,128)(2,1)S(1)}, u32[]{:S(2)}, u32[]{:S(2)}) collective-permute-start(bf16[512,256]{1,0:T(8,128)(2,1)S(1)} %collective-permute-done.1.refs_2_), channel_id=1, source_target_pairs={{0,1},{1,0},{2,3},{3,2},{4,5},{5,4},{6,7},{7,6},{8,9},{9,8},{10,11... | collective-permute-start | bytes 786440 | tf_op jit(solution)/shard_map/ppermute | solution.py:598
  15.4 35.2 %collective-permute-start.5 = (bf16[512,256]{1,0:T(8,128)(2,1)}, bf16[512,256]{1,0:T(8,128)(2,1)S(1)}, u32[]{:S(2)}, u32[]{:S(2)}) collective-permute-start(bf16[512,256]{1,0:T(8,128)(2,1)} %get-tuple-element.92.refs_0_), channel_id=1, source_target_pairs={{0,3},{1,2},{2,1},{3,0},{4,7},{5,6},{6,5},{7,4},{8,11},{9,10},{10,... | collective-permute-start | bytes 786440 | tf_op jit(solution)/shard_map/ppermute | solution.py:598
  17.1 33.9 %collective-permute-start.4 = (bf16[512,256]{1,0:T(8,128)(2,1)}, bf16[512,256]{1,0:T(8,128)(2,1)S(1)}, u32[]{:S(2)}, u32[]{:S(2)}) collective-permute-start(bf16[512,256]{1,0:T(8,128)(2,1)} %get-tuple-element.92.refs_0_), channel_id=1, source_target_pairs={{0,2},{1,3},{2,0},{3,1},{4,6},{5,7},{6,4},{7,5},{8,10},{9,11},{10,... | collective-permute-start | bytes 786440 | tf_op jit(solution)/shard_map/ppermute | solution.py:598
  17.4 33.6 %collective-permute-start.3 = (bf16[512,256]{1,0:T(8,128)(2,1)}, bf16[512,256]{1,0:T(8,128)(2,1)S(1)}, u32[]{:S(2)}, u32[]{:S(2)}) collective-permute-start(bf16[512,256]{1,0:T(8,128)(2,1)} %get-tuple-element.92.refs_0_), channel_id=1, source_target_pairs={{0,1},{1,0},{2,3},{3,2},{4,5},{5,4},{6,7},{7,6},{8,9},{9,8},{10,11... | collective-permute-start | bytes 786440 | tf_op jit(solution)/shard_map/ppermute | solution.py:598
  17.4 79.4 %all-to-all-start = ((f32[32,8,128]{2,1,0:T(8,128)}), f32[32,8,128]{2,1,0:T(8,128)S(1)}, u32[]{:S(2)}, u32[]{:S(2)}) async-start(f32[32,8,128]{2,1,0:T(8,128)} %get-tuple-element.115), calls=%async_computation | async-start | bytes 262144 | tf_op jit(solution)/shard_map/all_to_all | solution.py:621
  24.3 1.9 copy-start.4
  24.3 49.8 %collective-permute-start.8 = (bf16[512,256]{1,0:T(8,128)(2,1)}, bf16[512,256]{1,0:T(8,128)(2,1)S(1)}, u32[]{:S(2)}, u32[]{:S(2)}) collective-permute-start(bf16[512,256]{1,0:T(8,128)(2,1)} %get-tuple-element.103.refs_0_), channel_id=1, source_target_pairs={{0,3},{1,2},{2,1},{3,0},{4,7},{5,6},{6,5},{7,4},{8,11},{9,10},{10,... | collective-permute-start | bytes 786440 | tf_op jit(solution)/shard_map/ppermute | solution.py:598
  25.9 0.7 copy-start.5
  25.9 48.3 %collective-permute-start.7 = (bf16[512,256]{1,0:T(8,128)(2,1)}, bf16[512,256]{1,0:T(8,128)(2,1)S(1)}, u32[]{:S(2)}, u32[]{:S(2)}) collective-permute-start(bf16[512,256]{1,0:T(8,128)(2,1)} %get-tuple-element.103.refs_0_), channel_id=1, source_target_pairs={{0,2},{1,3},{2,0},{3,1},{4,6},{5,7},{6,4},{7,5},{8,10},{9,11},{10,... | collective-permute-start | bytes 786440 | tf_op jit(solution)/shard_map/ppermute | solution.py:598
  26.6 24.0 %copy-start.9 = (bf16[512,256]{1,0:T(8,128)(2,1)S(1)}, bf16[512,256]{1,0:T(8,128)(2,1)}, u32[]{:S(2)}) copy-start(bf16[512,256]{1,0:T(8,128)(2,1)} %get-tuple-element.103.refs_0_) | copy-start | bytes 786436
  50.5 0.7 copy-start.6
  50.6 23.7 %collective-permute-start.6 = (bf16[512,256]{1,0:T(8,128)(2,1)S(1)}, bf16[512,256]{1,0:T(8,128)(2,1)S(1)}, u32[]{:S(2)}, u32[]{:S(2)}) collective-permute-start(bf16[512,256]{1,0:T(8,128)(2,1)S(1)} %copy-done.9), channel_id=1, source_target_pairs={{0,1},{1,0},{2,3},{3,2},{4,5},{5,4},{6,7},{7,6},{8,9},{9,8},{10,11... | collective-permute-start | bytes 786440 | tf_op jit(solution)/shard_map/ppermute | solution.py:598
  51.0 0.7 copy-start.7
  51.0 0.8 copy-start.8
  74.2 0.7 copy-start.10
  74.2 0.8 copy-start.11
  74.2 0.8 copy-start.12
  96.9 0.7 copy-start.1
  149.3 58.4 %copy-start = (bf16[8,4,64,256]{3,2,1,0:T(8,128)(2,1)S(1)}, bf16[8,4,64,256]{3,2,1,0:T(8,128)(2,1)}, u32[]{:S(2)}) copy-start(bf16[8,4,64,256]{3,2,1,0:T(8,128)(2,1)} %get-tuple-element.121) | copy-start | bytes 3145732
  237.4 29.9 %all-to-all-start.3 = ((bf16[32,64,256]{2,1,0:T(8,128)(2,1)}), bf16[32,64,256]{2,1,0:T(8,128)(2,1)S(1)}, u32[]{:S(2)}, u32[]{:S(2)}) async-start(bf16[32,64,256]{2,1,0:T(8,128)(2,1)} %bitcast.24), calls=%async_computation.3 | async-start | bytes 2097152 | tf_op jit(solution)/shard_map/all_to_all | solution.py:784
  268.1 18.4 %all-to-all-start.6 = ((f32[8,64,256]{2,1,0:T(8,128)}), f32[8,64,256]{2,1,0:T(8,128)S(1)}, u32[]{:S(2)}, u32[]{:S(2)}) async-start(f32[8,64,256]{2,1,0:T(8,128)} %broadcast_in_dim.8), calls=%async_computation.6 | async-start | bytes 1048576 | tf_op jit(solution)/shard_map/all_to_all | solution.py:787
  287.3 18.3 %all-to-all-start.4 = ((f32[8,64,256]{2,1,0:T(8,128)}), f32[8,64,256]{2,1,0:T(8,128)S(1)}, u32[]{:S(2)}, u32[]{:S(2)}) async-start(f32[8,64,256]{2,1,0:T(8,128)} %broadcast_in_dim.7), calls=%async_computation.4 | async-start | bytes 1048576 | tf_op jit(solution)/shard_map/all_to_all | solution.py:787
